TPU v7x, 256 devices: a whole 4x4x8 slice. The times are simulated.
256 devices in a mesh: shard: 64 (over z, y_hi, x), heads: 2 (over y_lo), tensor: 2 (over core).
Axes of the slice: x: 4, y: 4 (y_hi: 2, y_lo: 2; y = y_hi * 2 + y_lo), z: 8, core: 2. Of those that a mesh axis runs over, the one named last changes fastest.
Arguments:
- noisy_patches: bfloat16 [256, 4096], P('shard'), may hold values from -6 to 6
- true_noise: bfloat16 [256, 4096], P('shard'), may hold values from -10 to 10
- timesteps: int32 [256], P('shard'), may hold values from 0 to 999
- labels: int32 [256], P('shard'), may hold values from 0 to 999
- attn_w: float32 [4, 1024, 1024], P(None, 'shard', 'heads'), may hold values from -2 to 2
- attn_mom: float32 [4, 1024, 1024], P(None, 'shard', 'heads'), may hold values from -1.1444092e-05 to 1.1444092e-05
- mlp_w: float32 [8, 1024, 1024], P(None, 'shard', 'tensor'), may hold values from -2 to 2
- mlp_mom: float32 [8, 1024, 1024], P(None, 'shard', 'tensor'), may hold values from -1.1444092e-05 to 1.1444092e-05
- mod_w: float32 [8, 1024, 1024], P(None, 'shard'), may hold values from -0.1875 to 0.1875
- mod_mom: float32 [8, 1024, 1024], P(None, 'shard'), may hold values from -1.1444092e-05 to 1.1444092e-05
- temb_w: float32 [1024, 1280], P('shard'), may hold values from -2 to 2
- temb_mom: float32 [1024, 1280], P('shard'), may hold values from -1.1444092e-05 to 1.1444092e-05
- label_table: float32 [1000, 1024], P(None, ('shard', 'heads', 'tensor')), may hold values from -6 to 6
- table_first: float32 [1000, 1024], P(None, ('shard', 'heads', 'tensor')), may hold values from -5.9604645e-07 to 5.9604645e-07
- table_second: float32 [1000, 1024], P(None, ('shard', 'heads', 'tensor')), may hold values from 9.536743e-15 to 3.8146972e-14
- io_w: float32 [2, 16, 1024], P(None, None, ('shard', 'heads', 'tensor')), may hold values from -2 to 2
- io_first: float32 [2, 16, 1024], P(None, None, ('shard', 'heads', 'tensor')), may hold values from -4.5776367e-05 to 4.5776367e-05
- io_second: float32 [2, 16, 1024], P(None, None, ('shard', 'heads', 'tensor')), may hold values from 6.1035156e-11 to 2.4414062e-10
- vec_w: float32 [19, 1024], P(None, ('shard', 'heads', 'tensor')), may hold values from -1.25 to 1.25
- vec_first: float32 [19, 1024], P(None, ('shard', 'heads', 'tensor')), may hold values from -4.5776367e-05 to 4.5776367e-05
- vec_second: float32 [19, 1024], P(None, ('shard', 'heads', 'tensor')), may hold values from 6.1035156e-11 to 2.4414062e-10
- head_b: float32 [16], replicated, may hold values from -1.25 to 1.25
- headb_first: float32 [16], replicated, may hold values from -0.00012207031 to 0.00012207031
- headb_second: float32 [16], replicated, may hold values from 3.8146972e-10 to 1.5258789e-09
Outputs:
- loss: float32 [], replicated
- grad_norm: float32 [], replicated
- attn_new: float32 [4, 1024, 1024], P(None, 'shard', 'heads')
- attn_moment: float32 [4, 1024, 1024], P(None, 'shard', 'heads')
- attn_copy: bfloat16 [4, 1024, 1024], P(None, 'shard', 'heads')
- mlp_new: float32 [8, 1024, 1024], P(None, 'shard', 'tensor')
- mlp_moment: float32 [8, 1024, 1024], P(None, 'shard', 'tensor')
- mlp_copy: bfloat16 [8, 1024, 1024], P(None, 'shard', 'tensor')
- mod_new: float32 [8, 1024, 1024], P(None, 'shard')
- mod_moment: float32 [8, 1024, 1024], P(None, 'shard')
- mod_copy: bfloat16 [8, 1024, 1024], P(None, 'shard')
- temb_new: float32 [1024, 1280], P('shard')
- temb_moment: float32 [1024, 1280], P('shard')
- table_new: float32 [1000, 1024], P(None, ('shard', 'heads', 'tensor'))
- table_first_new: float32 [1000, 1024], P(None, ('shard', 'heads', 'tensor'))
- table_second_new: float32 [1000, 1024], P(None, ('shard', 'heads', 'tensor'))
- table_copy: bfloat16 [1000, 1024], P(None, ('shard', 'heads', 'tensor'))
- io_new: float32 [2, 16, 1024], P(None, None, ('shard', 'heads', 'tensor'))
- io_first_new: float32 [2, 16, 1024], P(None, None, ('shard', 'heads', 'tensor'))
- io_second_new: float32 [2, 16, 1024], P(None, None, ('shard', 'heads', 'tensor'))
- vec_new: float32 [19, 1024], P(None, ('shard', 'heads', 'tensor'))
- vec_first_new: float32 [19, 1024], P(None, ('shard', 'heads', 'tensor'))
- vec_second_new: float32 [19, 1024], P(None, ('shard', 'heads', 'tensor'))
- headb_new: float32 [16], replicated
- headb_first_new: float32 [16], replicated
- headb_second_new: float32 [16], replicated
All inputs are finite; a program needn't handle non-finite values.
Results may differ from a plain program's by a relative error of at most 0.0091.
Values may be sent and summed in bfloat16 or wider, within the bound.
No kernel may reach another device: no remote copies, remote signals or barrier semaphores. Data moves between devices by JAX's collectives and lax.ppermute only.
A program may use at most 320 MiB of HBM per device.

v0:
```python
import functools
import math

import jax
import jax.numpy as jnp
from jax import lax
from jax.experimental import pallas as pl
from jax.experimental.pallas import tpu as pltpu
from jax.sharding import Mesh
from jax.sharding import PartitionSpec as P

D = 1024
HDIM = 64
FREQ = 256
NCLS = 1000
PATCH = 16
GRID = 16
SEQ = 256
RB = 16
NS_STEPS = 5
STEP = 10
SHARD_SIZES = (8, 2, 4)
INTERPRET = False

HIGH = lax.Precision.HIGHEST
NS_A = 3.4445
NS_B = -4.775
NS_C = 2.0315
CLIP_NORM = 0.01
LR_MUON = 0.5
MOMENT_DECAY = 0.5
BETA_ONE = 0.5
BETA_TWO = 0.5
ADAM_EPS = 1e-08
LN_EPS = 1e-06

BF = jnp.bfloat16
F32 = jnp.float32

SHARD = ("z", "yh", "x")
PLANE = ("yh", "x", "yl")
ALL = ("z", "yh", "x", "yl", "c")


def dot(lhs, rhs, lhs_dim, rhs_dim, precision=None):
    return lax.dot_general(
        lhs,
        rhs,
        (((lhs_dim,), (rhs_dim,)), ((), ())),
        precision=precision,
        preferred_element_type=F32,
    )


def rounded(v):
    return lax.reduce_precision(v.astype(F32), 8, 7)


def exchange(v, axes):
    return lax.all_to_all(v, axes, 0, 0, tiled=True)


def swap(v, axis):
    return lax.ppermute(v, axis, [(0, 1), (1, 0)])


def in_order(index, mine, other, axis):
    return jnp.where(
        index == 0,
        jnp.concatenate([mine, other], axis=axis),
        jnp.concatenate([other, mine], axis=axis),
    )


def grid_table():
    quarter = D // 4
    rates = jnp.exp(-math.log(10000.0) * jnp.arange(quarter, dtype=F32) / quarter)
    phases = jnp.arange(GRID).astype(F32)[:, None] * rates[None, :]
    sines, cosines = jnp.sin(phases), jnp.cos(phases)
    full = (GRID, GRID, quarter)
    return jnp.concatenate(
        [
            jnp.broadcast_to(sines[None], full),
            jnp.broadcast_to(cosines[None], full),
            jnp.broadcast_to(sines[:, None], full),
            jnp.broadcast_to(cosines[:, None], full),
        ],
        axis=2,
    ).reshape(SEQ, D)


def layer_norm(values):
    center = jnp.mean(values, axis=-1, keepdims=True)
    shifted = values - center
    inv_std = lax.rsqrt(jnp.mean(shifted * shifted, axis=-1, keepdims=True) + LN_EPS)
    return (shifted * inv_std, inv_std)


def norm_back(grad_norm, normed, inv_std):
    return inv_std * (
        grad_norm
        - jnp.mean(grad_norm, axis=-1, keepdims=True)
        - normed * jnp.mean(grad_norm * normed, axis=-1, keepdims=True)
    )


def gelu_tanh(values):
    return jax.nn.gelu(values, approximate=True)


def newton_kernel(gram_ref, norm_ref, out_ref):
    size = gram_ref.shape[-1]
    rows = lax.broadcasted_iota(jnp.int32, (size, size), 0)
    cols = lax.broadcasted_iota(jnp.int32, (size, size), 1)
    eye = (rows == cols).astype(F32)
    groups = gram_ref.shape[0]
    inv = [1.0 / norm_ref[g] for g in range(groups)]
    quad = [gram_ref[g] * (inv[g] * inv[g]) for g in range(groups)]
    total = [None] * groups

    def mul(a, b):
        return jnp.dot(a, b, precision=HIGH, preferred_element_type=F32)

    for turn in range(NS_STEPS):
        poly = [NS_A * eye + NS_B * q + NS_C * mul(q, q) for q in quad]
        total = [p if turn == 0 else mul(p, t) for p, t in zip(poly, total)]
        if turn < NS_STEPS - 1:
            half = [mul(p, q) for p, q in zip(poly, quad)]
            quad = [mul(h, p) for h, p in zip(half, poly)]
    for g in range(groups):
        out_ref[g] = total[g] * inv[g]


def newton_maps(grams):
    size = 8 * RB
    groups = grams.shape[0] // 8
    norms = jnp.sqrt(jnp.einsum("bii->b", grams)) + 1e-07
    place = jnp.arange(size) // RB
    same = (place[:, None] == place[None, :])[None]
    tiled = jnp.tile(grams.reshape(groups, size, RB), (1, 1, 8))
    blocks = jnp.where(same, tiled, 0.0)
    norm_rows = jnp.broadcast_to(
        jnp.repeat(norms, RB).reshape(groups, size, 1), (groups, size, size)
    )
    return pl.pallas_call(
        newton_kernel,
        out_shape=jax.ShapeDtypeStruct((groups, size, size), F32),
        interpret=INTERPRET,
    )(blocks, norm_rows)


def adam(weight, first_old, second_old, grad_in, step_rate):
    first_new = BETA_ONE * first_old + (1.0 - BETA_ONE) * grad_in
    second_new = BETA_TWO * second_old + (1.0 - BETA_TWO) * grad_in * grad_in
    fix_one = 1.0 - BETA_ONE**STEP
    fix_two = 1.0 - BETA_TWO**STEP
    new_weight = weight - step_rate * (first_new / fix_one) / (
        jnp.sqrt(second_new / fix_two) + ADAM_EPS
    )
    return (new_weight, first_new, second_new)


def heads_of(v):
    return v.reshape(SEQ, -1, HDIM)


def raw_scores(q_low, k_low):
    return jnp.einsum(
        "qhd,khd->hqk", heads_of(q_low), heads_of(k_low), preferred_element_type=F32
    ) * (1.0 / math.sqrt(HDIM))


def attend(q_low, k_low, v_low):
    scores = raw_scores(q_low, k_low)
    peak = jnp.max(scores, axis=-1, keepdims=True)
    log_total = peak + jnp.log(jnp.sum(jnp.exp(scores - peak), axis=-1, keepdims=True))
    probs = jnp.exp(scores - log_total).astype(BF)
    out = jnp.einsum("hqk,khd->qhd", probs, heads_of(v_low), preferred_element_type=F32)
    return out.reshape(q_low.shape).astype(BF), log_total


def attend_back(q_low, k_low, v_low, log_total, d_att):
    shape = q_low.shape
    probs = jnp.exp(raw_scores(q_low, k_low) - log_total)
    d_heads = heads_of(d_att)
    d_probs = jnp.einsum("qhd,khd->hqk", d_heads, heads_of(v_low), preferred_element_type=F32)
    d_value = jnp.einsum("hqk,qhd->khd", probs.astype(BF), d_heads, preferred_element_type=F32)
    row_dot = jnp.sum(d_probs * probs, axis=-1, keepdims=True)
    d_raw = (probs * (d_probs - row_dot) * (1.0 / math.sqrt(HDIM))).astype(BF)
    d_query = jnp.einsum("hqk,khd->qhd", d_raw, heads_of(k_low), preferred_element_type=F32)
    d_key = jnp.einsum("hqk,qhd->khd", d_raw, heads_of(q_low), preferred_element_type=F32)
    return (
        d_query.reshape(shape).astype(BF),
        d_key.reshape(shape).astype(BF),
        d_value.reshape(shape).astype(BF),
    )


def on_device(
    noisy_patches,
    true_noise,
    timesteps,
    labels,
    attn_w,
    attn_mom,
    mlp_w,
    mlp_mom,
    mod_w,
    mod_mom,
    temb_w,
    temb_mom,
    label_table,
    table_first,
    table_second,
    io_w,
    io_first,
    io_second,
    vec_w,
    vec_first,
    vec_second,
    head_b,
    headb_first,
    headb_second,
):
    n_shard = lax.axis_size(SHARD)
    n_all = lax.axis_size(ALL)
    n_plane = lax.axis_size(PLANE)
    count_all = n_all * SEQ * PATCH
    yl, core = lax.axis_index("yl"), lax.axis_index("c")
    sub = 2 * yl + core
    shard = lax.axis_index(SHARD)
    half = D // 2
    quarter = D // 4
    wide = 4 * half

    attn_low = lax.dynamic_slice_in_dim(attn_w, core * quarter, quarter, axis=2).astype(BF)
    mlp_low = lax.dynamic_slice_in_dim(mlp_w, yl * 4, 4, axis=0).astype(BF)
    own_rows = jnp.concatenate(
        [
            attn_low.transpose(1, 0, 2).reshape(RB, 4 * quarter),
            mlp_low.transpose(1, 0, 2).reshape(RB, wide),
        ],
        axis=1,
    )
    plane_rows = exchange(
        jnp.broadcast_to(own_rows[None], (n_plane,) + own_rows.shape), PLANE
    ).reshape(n_plane // 2, 2, RB, -1)
    z_rows = n_plane // 2 * RB
    attn_z = (
        plane_rows[..., : 4 * quarter]
        .reshape(n_plane // 2, 2, RB, 4, quarter)
        .transpose(0, 2, 3, 1, 4)
        .reshape(z_rows, wide)
    )
    first_z = plane_rows[:, 0, :, 4 * quarter :].reshape(z_rows, wide)
    second_z = plane_rows[:, 1, :, 4 * quarter :].reshape(z_rows, wide)
    attn_mine = lax.all_gather(attn_z, "z", axis=0, tiled=True)
    first_mine = lax.all_gather(first_z, "z", axis=0, tiled=True)
    second_mine = lax.all_gather(second_z, "z", axis=0, tiled=True)
    attn_halves = (attn_mine, swap(attn_mine, "c"))
    first_halves = (first_mine, swap(first_mine, "c"))
    second_halves = (second_mine, swap(second_mine, "c"))

    label_own = lax.dynamic_index_in_dim(labels, sub, keepdims=False)
    time_own = lax.dynamic_index_in_dim(timesteps, sub, keepdims=False)
    vec_cols = vec_w.shape[1]
    lanes_io = vec_w.shape[0]
    lanes_int = lanes_io + 2 * PATCH
    lanes_mod = 64
    lanes_all = 128
    ints = jnp.stack([label_own // 32, label_own % 32, time_own // 32, time_own % 32])
    common = jnp.concatenate(
        [
            vec_w.T.astype(BF),
            io_w.reshape(2 * PATCH, vec_cols).T.astype(BF),
            jnp.broadcast_to(ints.astype(BF)[None], (vec_cols, 4)),
            jnp.zeros((vec_cols, lanes_mod - lanes_int - 4), BF),
        ],
        axis=1,
    )
    mod_own = mod_w.astype(BF)
    mod_cols = (
        lax.dynamic_slice_in_dim(mod_own, sub * 4, 4, axis=1)
        .reshape(4, 2, 4, n_shard, RB)
        .transpose(3, 0, 2, 1, 4)
        .reshape(n_all, 4, 2 * RB)
    )
    sent = jnp.concatenate(
        [
            jnp.broadcast_to(common[None], (n_all,) + common.shape),
            mod_cols,
            jnp.zeros((n_all, 4, lanes_all - lanes_mod - 2 * RB), BF),
        ],
        axis=2,
    )
    got = exchange(sent, ALL)
    marks = got[:, 0, lanes_int : lanes_int + 4].astype(F32)
    labels_all = (marks[:, 0] * 32.0 + marks[:, 1]).astype(jnp.int32)
    times_all = marks[:, 2] * 32.0 + marks[:, 3]
    by_feature = got.reshape(D, lanes_all)
    by_row = by_feature[:, :lanes_int].astype(F32).T
    vec_f = by_row[:lanes_io]
    io_low = by_row[lanes_io:lanes_int].astype(BF)
    mod_col = by_feature[:, lanes_mod : lanes_mod + 2 * RB]
    own_features = lax.dynamic_slice_in_dim(by_feature, shard * RB, RB, axis=0)[
        :, :lanes_io
    ].astype(F32)
    own_mod_bias = lax.dynamic_slice_in_dim(own_features, 3 + 2 * sub, 2, axis=1)

    rates = jnp.exp(-math.log(10000.0) * jnp.arange(FREQ // 2, dtype=F32) / (FREQ // 2))
    phases = rates[:, None] * times_all[None, :]
    freq_t = jnp.concatenate([jnp.cos(phases), jnp.sin(phases)], axis=0).astype(BF)
    temb_low = temb_w.astype(BF)
    pre_t = dot(temb_low[:, :FREQ], freq_t, 1, 0) + own_features[:, 1:2]
    hid_t = jax.nn.silu(pre_t).astype(BF)
    temb_cols = lax.dynamic_slice_in_dim(
        temb_low[:, FREQ:].reshape(RB, n_shard, 4, vec_cols), sub, 1, axis=2
    ).reshape(RB, n_shard * vec_cols)
    cond_parts = dot(temb_cols, hid_t, 0, 0)
    cond_parts = exchange(cond_parts.reshape(n_shard, vec_cols, n_all), SHARD)
    onehot = (labels_all[:, None] == jnp.arange(NCLS)[None, :]).astype(BF)
    label_rows = dot(label_table.astype(BF), onehot, 0, 1)
    cond_t = jnp.sum(cond_parts, axis=0) + label_rows + rounded(vec_w[2])[:, None]
    act_own = jax.nn.silu(cond_t).astype(BF)
    act_t = exchange(jnp.broadcast_to(act_own[None], (n_all,) + act_own.shape), ALL).reshape(
        D, n_all
    )
    mods_sent = dot(act_t, mod_col, 0, 0) + own_mod_bias.T.reshape(1, 2 * RB)
    mods = (
        exchange(mods_sent, ALL)
        .reshape(n_shard, 8, RB)
        .transpose(1, 0, 2)
        .reshape(8, 1, D)
    )

    patch_vals = lax.dynamic_index_in_dim(noisy_patches, sub, keepdims=False).reshape(SEQ, PATCH)
    target = lax.dynamic_index_in_dim(true_noise, sub, keepdims=False).reshape(SEQ, PATCH)
    head_low = rounded(head_b)
    x_in = dot(patch_vals, io_low[:PATCH], 1, 0) + vec_f[0] + grid_table()
    norm_one, inv_one = layer_norm(x_in)
    h_one = (norm_one * (1.0 + mods[1]) + mods[0]).astype(BF)
    own_half = (core, 1 - core)

    def attn_bias(row, which):
        rows = vec_f[row].reshape(2, 2, quarter)
        return lax.dynamic_index_in_dim(rows, which, axis=1, keepdims=False).reshape(half)

    qkv = []
    attended = []
    log_totals = []
    attn_out = vec_f[13]
    for weight, which in zip(attn_halves, own_half):
        proj = dot(h_one, weight[:, : 3 * half], 1, 0)
        q_low = (proj[:, :half] + attn_bias(11, which)).astype(BF)
        k_low = proj[:, half : 2 * half].astype(BF)
        v_low = (proj[:, 2 * half :] + attn_bias(12, which)).astype(BF)
        att, log_total = attend(q_low, k_low, v_low)
        qkv.append((q_low, k_low, v_low))
        attended.append(att)
        log_totals.append(log_total)
        attn_out = attn_out + dot(att, weight[:, 3 * half :], 1, 1)
    x_one = x_in + mods[2] * attn_out
    norm_two, inv_two = layer_norm(x_one)
    h_two = (norm_two * (1.0 + mods[4]) + mods[3]).astype(BF)
    pre_mlp = []
    act_mlp = []
    mlp_out = vec_f[18]
    for first, second, which in zip(first_halves, second_halves, own_half):
        bias = lax.dynamic_slice_in_dim(vec_f[14:18], which * half, half, axis=1).reshape(wide)
        pre = dot(h_two, first, 1, 0) + bias
        act = gelu_tanh(pre).astype(BF)
        pre_mlp.append(pre)
        act_mlp.append(act)
        mlp_out = mlp_out + dot(act, second, 1, 1)
    x_two = x_one + mods[5] * mlp_out
    norm_fin, inv_fin = layer_norm(x_two)
    y_low = (norm_fin * (1.0 + mods[7]) + mods[6]).astype(BF)
    pred_error = dot(y_low, io_low[PATCH:], 1, 1) + head_low - target.astype(F32)
    loss_own = jnp.sum(pred_error * pred_error)

    d_pred = pred_error * (2.0 / count_all)
    d_pred_low = d_pred.astype(BF)
    grad_head = dot(d_pred_low, y_low, 0, 0)
    grad_hb = jnp.sum(d_pred, axis=0)
    d_y = dot(d_pred_low, io_low[PATCH:], 1, 0)
    d_shift_fin = jnp.sum(d_y, axis=0)
    d_scale_fin = jnp.sum(d_y * norm_fin, axis=0)
    d_two = norm_back(d_y * (1.0 + mods[7]), norm_fin, inv_fin)
    d_gate_two = jnp.sum(d_two * mlp_out, axis=0)
    d_mlp = mods[5] * d_two
    d_mlp_low = d_mlp.astype(BF)
    grad_bfc = jnp.sum(d_mlp, axis=0)
    grad_second = [dot(d_mlp_low, act, 0, 0).astype(BF) for act in act_mlp]
    second_sum = chip_sum(grad_second)
    second_z = lax.psum_scatter(second_sum, "z", scatter_dimension=0, tiled=True)
    d_pre_low = []
    hid_bias = []
    d_h_two = 0.0
    for pre, first, second in zip(pre_mlp, first_halves, second_halves):
        d_act = dot(d_mlp_low, second, 1, 0)
        d_pre = jax.vjp(gelu_tanh, pre)[1](d_act)[0]
        hid_bias.append(jnp.sum(d_pre, axis=0).reshape(4, half))
        d_pre_low.append(d_pre.astype(BF))
        d_h_two = d_h_two + dot(d_pre_low[-1], first, 1, 1)
    grad_first = [dot(h_two, d, 0, 0).astype(BF) for d in d_pre_low]
    first_sum = chip_sum(grad_first)
    first_z = lax.psum_scatter(first_sum, "z", scatter_dimension=0, tiled=True)
    grad_bhid = in_order(core, hid_bias[0], hid_bias[1], 1)
    d_shift_two = jnp.sum(d_h_two, axis=0)
    d_scale_two = jnp.sum(d_h_two * norm_two, axis=0)
    d_one = d_two + norm_back(d_h_two * (1.0 + mods[4]), norm_two, inv_two)
    d_gate_one = jnp.sum(d_one * attn_out, axis=0)
    d_attn = mods[2] * d_one
    d_attn_low = d_attn.astype(BF)
    grad_bout = jnp.sum(d_attn, axis=0)
    grad_attn = []
    qv_bias = []
    d_h_one = 0.0
    for weight, (q_low, k_low, v_low), att, log_total in zip(
        attn_halves, qkv, attended, log_totals
    ):
        d_att = dot(d_attn_low, weight[:, 3 * half :], 1, 0).astype(BF)
        d_query, d_key, d_value = attend_back(q_low, k_low, v_low, log_total, d_att)
        d_proj = jnp.concatenate([d_query, d_key, d_value], axis=1)
        grad_attn.append(
            jnp.concatenate(
                [
                    dot(h_one, d_proj, 0, 0).astype(BF),
                    dot(d_attn_low, att, 0, 0).astype(BF),
                ],
                axis=1,
            )
        )
        qv_bias.append(
            jnp.stack(
                [
                    jnp.sum(d_query.astype(F32), axis=0),
                    jnp.sum(d_value.astype(F32), axis=0),
                ]
            ).reshape(2, 2, 1, quarter)
        )
        d_h_one = d_h_one + dot(d_proj, weight[:, : 3 * half], 1, 1)
    attn_sum = chip_sum(grad_attn)
    attn_zg = lax.psum_scatter(attn_sum, "z", scatter_dimension=0, tiled=True)
    grad_bqv = in_order(core, qv_bias[0], qv_bias[1], 2).reshape(2, D)
    d_shift_one = jnp.sum(d_h_one, axis=0)
    d_scale_one = jnp.sum(d_h_one * norm_one, axis=0)
    d_in = d_one + norm_back(d_h_one * (1.0 + mods[1]), norm_one, inv_one)
    grad_patch = dot(patch_vals, d_in.astype(BF), 0, 0)
    grad_bpatch = jnp.sum(d_in, axis=0)
    d_mods = jnp.stack(
        [
            d_shift_one,
            d_scale_one,
            d_gate_one,
            d_shift_two,
            d_scale_two,
            d_gate_two,
            d_shift_fin,
            d_scale_fin,
        ]
    )

    dmod_sent = jnp.broadcast_to(
        d_mods.astype(BF).reshape(1, 4, 2 * D), (n_shard, 4, 2 * D)
    ).reshape(n_all, 2 * D)
    dmod_all = exchange(dmod_sent, ALL)
    mod_sub = lax.dynamic_slice_in_dim(mod_own, 2 * sub, 2, axis=0)
    act_rows = lax.dynamic_slice_in_dim(act_t, shard * RB, RB, axis=0)
    grad_mod = dot(act_rows, dmod_all, 1, 0).reshape(RB, 2, D).transpose(1, 0, 2)
    d_act = dot(mod_sub.transpose(1, 0, 2).reshape(RB, 2 * D), dmod_all, 1, 1)
    d_act = lax.psum(d_act, ("yl", "c"))
    d_act = lax.dynamic_slice_in_dim(d_act, sub * vec_cols, vec_cols, axis=0)
    d_cond = jax.vjp(jax.nn.silu, cond_t)[1](d_act)[0]
    grad_table = dot(onehot.astype(F32), d_cond, 0, 1, HIGH)
    grad_bt_two = jnp.sum(d_cond, axis=1)
    d_cond_low = d_cond.astype(BF)
    d_cond_t = exchange(
        jnp.broadcast_to(d_cond_low[None], (n_all,) + d_cond_low.shape), ALL
    ).reshape(D, n_all)
    d_hidden = dot(temb_low[:, FREQ:], d_cond_t, 1, 0)
    d_pre_time = jax.vjp(jax.nn.silu, pre_t)[1](d_hidden)[0]
    grad_bt_one = lax.dynamic_slice_in_dim(
        jnp.sum(d_pre_time, axis=1), sub * vec_cols, vec_cols, axis=0
    )
    grad_temb = jnp.concatenate(
        [dot(d_pre_time.astype(BF), freq_t, 1, 1), dot(hid_t, d_cond_t, 1, 1)], axis=1
    )

    small = jnp.concatenate(
        [
            grad_bpatch[None],
            d_mods,
            grad_bqv,
            grad_bout[None],
            grad_bhid,
            grad_bfc[None],
            grad_patch,
            grad_head,
        ],
        axis=0,
    )
    n_small = small.shape[0]
    small_sent = (
        jnp.pad(small, ((0, 64 - n_small), (0, 0))).T.reshape(n_all, vec_cols, 64)
    )
    small_own = jnp.sum(exchange(small_sent, ALL), axis=0).T
    vec_s = jnp.concatenate(
        [small_own[:1], grad_bt_one[None], grad_bt_two[None], small_own[1:17]], axis=0
    )
    io_s = small_own[17:n_small].reshape(2, PATCH, vec_cols)

    grads_sent = jnp.concatenate(
        [
            attn_zg.reshape(n_plane // 2, RB, 4, 2, quarter)
            .transpose(0, 3, 1, 2, 4)
            .reshape(n_plane // 2, 2, RB, 4 * quarter),
            jnp.stack(
                [
                    first_z.reshape(n_plane // 2, RB, wide),
                    second_z.reshape(n_plane // 2, RB, wide),
                ],
                axis=1,
            ),
        ],
        axis=3,
    ).reshape(n_plane, RB, 4 * quarter + wide)
    grads_own = jnp.sum(exchange(grads_sent, PLANE).astype(F32), axis=0)
    attn_q = grads_own[:, : 4 * quarter].reshape(RB, 4, quarter).transpose(1, 0, 2)
    mlp_q = grads_own[:, 4 * quarter :].reshape(RB, 4, half).transpose(1, 0, 2)
    attn_s = in_order(core, attn_q, swap(attn_q, "c"), 2)
    mlp_s = in_order(yl, mlp_q, swap(mlp_q, "yl"), 0)
    mod_s = lax.all_gather(
        lax.all_gather(grad_mod, "c", axis=0, tiled=True), "yl", axis=0, tiled=True
    )

    local_square = (
        jnp.sum(grads_own * grads_own)
        + jnp.sum(grad_mod * grad_mod)
        + 0.25 * jnp.sum(grad_temb * grad_temb)
        + jnp.sum(grad_table * grad_table)
        + jnp.sum(io_s * io_s)
        + jnp.sum(vec_s * vec_s)
    )
    sums = jnp.concatenate([local_square[None], loss_own[None], grad_hb])
    sums = jnp.pad(sums, (0, 128 - sums.shape[0]))
    sums = jnp.sum(exchange(jnp.broadcast_to(sums[None], (n_all, 128)), ALL), axis=0)
    loss = sums[1] / count_all
    head_all = sums[2 : 2 + PATCH]
    grad_norm = jnp.sqrt(sums[0] + jnp.sum(head_all * head_all))
    factor = jnp.minimum(1.0, CLIP_NORM / (grad_norm + 1e-06))

    attn_moment = MOMENT_DECAY * attn_mom + factor * attn_s
    mlp_moment = MOMENT_DECAY * mlp_mom + factor * mlp_s
    mod_moment = MOMENT_DECAY * mod_mom + factor * mod_s
    temb_moment = MOMENT_DECAY * temb_mom + factor * grad_temb
    gram_attn = jnp.einsum("bij,bkj->bik", attn_moment, attn_moment, precision=HIGH)
    gram_mlp = jnp.einsum("bij,bkj->bik", mlp_moment, mlp_moment, precision=HIGH)
    gram_mod = jnp.einsum("bij,bkj->bik", mod_moment, mod_moment, precision=HIGH)
    temb_left, temb_right = temb_moment[:, :FREQ], temb_moment[:, FREQ:]
    gram_left = dot(temb_left, temb_left, 1, 1, HIGH)[None]
    gram_right = dot(temb_right, temb_right, 1, 1, HIGH)[None]
    gram_attn = gram_attn + swap(gram_attn, "yl")
    gram_mlp = gram_mlp + swap(gram_mlp, "c")
    maps = newton_maps(
        jnp.concatenate(
            [gram_attn, gram_left, gram_right, jnp.zeros((2, RB, RB), F32), gram_mlp, gram_mod]
        )
    )
    n_attn = 4 * RB
    attn_ortho = dot(
        maps[0, :n_attn, :n_attn], attn_moment.reshape(n_attn, half), 1, 0, HIGH
    ).reshape(attn_moment.shape)
    left_ortho = dot(
        maps[0, n_attn : n_attn + RB, n_attn : n_attn + RB], temb_left, 1, 0, HIGH
    )
    right_ortho = dot(
        maps[0, n_attn + RB : n_attn + 2 * RB, n_attn + RB : n_attn + 2 * RB],
        temb_right,
        1,
        0,
        HIGH,
    )
    mlp_ortho = dot(maps[1], mlp_moment.reshape(8 * RB, half), 1, 0, HIGH).reshape(
        mlp_moment.shape
    )
    mod_ortho = dot(maps[2], mod_moment.reshape(8 * RB, D), 1, 0, HIGH).reshape(mod_moment.shape)
    attn_new = attn_w - LR_MUON * attn_ortho
    mlp_new = mlp_w - LR_MUON * mlp_ortho
    mod_new = mod_w - LR_MUON * mod_ortho
    temb_new = temb_w - LR_MUON * jnp.concatenate([left_ortho, right_ortho], axis=1)
    table_new, table_first_new, table_second_new = adam(
        label_table, table_first, table_second, factor * grad_table, 0.3
    )
    io_rates = jnp.array([0.1, 0.01], F32).reshape(2, 1, 1)
    io_new, io_first_new, io_second_new = adam(io_w, io_first, io_second, factor * io_s, io_rates)
    vec_new, vec_first_new, vec_second_new = adam(
        vec_w, vec_first, vec_second, factor * vec_s, 0.05
    )
    headb_new, headb_first_new, headb_second_new = adam(
        head_b, headb_first, headb_second, factor * head_all, 0.05
    )
    return (
        loss,
        grad_norm,
        attn_new,
        attn_moment,
        attn_new.astype(BF),
        mlp_new,
        mlp_moment,
        mlp_new.astype(BF),
        mod_new,
        mod_moment,
        mod_new.astype(BF),
        temb_new,
        temb_moment,
        table_new,
        table_first_new,
        table_second_new,
        table_new.astype(BF),
        io_new,
        io_first_new,
        io_second_new,
        vec_new,
        vec_first_new,
        vec_second_new,
        headb_new,
        headb_first_new,
        headb_second_new,
    )


def chip_sum(halves):
    mine, other = halves
    return (mine.astype(F32) + swap(other, "c").astype(F32)).astype(BF)


def solution(mesh):
    fine = Mesh(mesh.devices.reshape(SHARD_SIZES + (2, 2)), ALL)
    lat = P(SHARD, None)
    one = P(SHARD)
    attn = P(None, SHARD, "yl")
    mlp = P(None, SHARD, "c")
    mod = P(None, SHARD, None)
    temb = P(SHARD, None)
    flat = P(None, ALL)
    io = P(None, None, ALL)
    rep = P()
    return jax.shard_map(
        on_device,
        mesh=fine,
        in_specs=(lat, lat, one, one, attn, attn, mlp, mlp, mod, mod, temb, temb)
        + (flat,) * 3
        + (io,) * 3
        + (flat,) * 3
        + (rep,) * 3,
        out_specs=(rep, rep)
        + (attn,) * 3
        + (mlp,) * 3
        + (mod,) * 3
        + (temb,) * 2
        + (flat,) * 4
        + (io,) * 3
        + (flat,) * 3
        + (rep,) * 3,
        check_vma=False,
    )
```

profile of v0, /device:TPU:1, one launch (start us, length us, event | category | flops | bytes accessed | tf_op | source)
XLA Modules:
  0.0 643.2 jit_solution(14364851319521063450)
XLA Ops:
  9.3 29.0 %all_to_all.63 = bf16[16,16,3072]{2,1,0:T(8,128)(2,1)S(1)} all-to-all(bf16[16,16,3072]{2,1,0:T(8,128)(2,1)S(1)} %broadcast_in_dim.73), channel_id=1, replica_groups=mesh['z'=8,'yh'=2,'x'=4,'yl'=2,'c'=2] {'yh','x','yl'}, dimensions={0} | all-to-all | bytes 3145728 | tf_op jit(solution)/shard_map/all_to_all | solution.py:60
  52.6 12.7 %all-to-all-start = ((bf16[256,4,128]{2,1,0:T(4,128)(2,1)}), bf16[256,4,128]{2,1,0:T(4,128)(2,1)S(1)}, u32[]{:S(2)}, u32[]{:S(2)}) async-start(bf16[256,4,128]{2,1,0:T(4,128)(2,1)} %maximum_maximum_fusion), calls=%async_computation | async-start | bytes 524288 | tf_op jit(solution)/shard_map/all_to_all | solution.py:60
  66.0 16.9 %all-to-all-done = bf16[256,4,128]{2,1,0:T(4,128)(2,1)S(1)} async-done(((bf16[256,4,128]{2,1,0:T(4,128)(2,1)}), bf16[256,4,128]{2,1,0:T(4,128)(2,1)S(1)}, u32[]{:S(2)}, u32[]{:S(2)}) %all-to-all-start) | async-done | bytes 262176 | tf_op jit(solution)/shard_map/all_to_all | solution.py:60
  85.2 5.4 all-to-all-start.1
  93.1 14.6 %all-gather.4.cloned.1.call-done = bf16[1024,2048]{1,0:T(8,128)(2,1)} async-done(((bf16[128,2048]{1,0:T(8,128)(2,1)}), bf16[1024,2048]{1,0:T(8,128)(2,1)}) %all-gather.4.cloned.1.call-update) | async-done | bytes 4194320 | tf_op jit(solution)/shard_map/all_gather | solution.py:257
  112.1 10.5 %all-to-all-start.2 = ((bf16[256,4,256]{2,1,0:T(4,128)(2,1)}), bf16[256,4,256]{2,1,0:T(4,128)(2,1)S(1)}, u32[]{:S(2)}, u32[]{:S(2)}) async-start(bf16[256,4,256]{2,1,0:T(4,128)(2,1)} %broadcast_in_dim.72), calls=%async_computation.2 | async-start | bytes 1048576 | tf_op jit(solution)/shard_map/all_to_all | solution.py:60
  125.8 22.3 %all-to-all-done.2 = bf16[256,4,256]{2,1,0:T(4,128)(2,1)S(1)} async-done(((bf16[256,4,256]{2,1,0:T(4,128)(2,1)}), bf16[256,4,256]{2,1,0:T(4,128)(2,1)S(1)}, u32[]{:S(2)}, u32[]{:S(2)}) %all-to-all-start.2) | async-done | bytes 524320 | tf_op jit(solution)/shard_map/all_to_all | solution.py:60
  149.3 6.4 all-to-all-start.3
  156.4 13.3 %all-to-all-done.3 = f32[256,1,32]{2,1,0:T(1,128)S(1)} async-done(((f32[256,1,32]{2,1,0:T(1,128)}), f32[256,1,32]{2,1,0:T(1,128)S(1)}, u32[]{:S(2)}, u32[]{:S(2)}) %all-to-all-start.3) | async-done | bytes 32800 | tf_op jit(solution)/shard_map/all_to_all | solution.py:60
  184.7 48.1 %all-gather.8.cloned.1.call-done = bf16[1024,2048]{1,0:T(8,128)(2,1)} async-done(((bf16[128,2048]{1,0:T(8,128)(2,1)}), bf16[1024,2048]{1,0:T(8,128)(2,1)}) %all-gather.8.cloned.1.call-update) | async-done | bytes 4194320 | tf_op jit(solution)/shard_map/all_gather | solution.py:259
  273.0 5.5 fusion.177
  279.9 4.5 multiply_reduce_fusion.7
  297.6 5.4 fusion.48
  303.0 6.0 convert_reduce_fusion.2
  325.5 4.7 convert_reduce_fusion.4
  335.0 4.3 add_convert_fusion.2
  343.4 6.8 %collective-permute-done.4 = bf16[1024,2048]{1,0:T(8,128)(2,1)S(1)} collective-permute-done((bf16[1024,2048]{1,0:T(8,128)(2,1)S(1)}, bf16[1024,2048]{1,0:T(8,128)(2,1)S(1)}, u32[]{:S(2)}, u32[]{:S(2)}) %collective-permute-start.4) | collective-permute-done | bytes 4194336 | tf_op jit(solution)/shard_map/ppermute | solution.py:64
  358.4 6.8 %collective-permute-done.5 = bf16[1024,2048]{1,0:T(8,128)(2,1)S(1)} collective-permute-done((bf16[1024,2048]{1,0:T(8,128)(2,1)S(1)}, bf16[1024,2048]{1,0:T(8,128)(2,1)S(1)}, u32[]{:S(2)}, u32[]{:S(2)}) %collective-permute-start.5) | collective-permute-done | bytes 4194336 | tf_op jit(solution)/shard_map/ppermute | solution.py:64
  378.9 6.2 all_to_all.52
  385.6 7.8 %reduce.66 = bf16[256,2048]{1,0:T(8,128)(2,1)} reduce(bf16[256,1,2048]{2,1,0:T(2,128)(2,1)S(1)} %all_to_all.52, bf16[]{:T(256)} %broadcast.650), dimensions={1}, to_apply=%all_to_all.52.reduce_sub_computation | reduce | bytes 2097154 | tf_op jit(solution)/shard_map/all_to_all | solution.py:60
  396.2 11.1 %all-to-all-start.6 = ((bf16[256,2,1024]{2,1,0:T(2,128)(2,1)}), bf16[256,2,1024]{2,1,0:T(2,128)(2,1)}, u32[]{:S(2)}, u32[]{:S(2)}) async-start(bf16[256,2,1024]{2,1,0:T(2,128)(2,1)} %reshape.741), calls=%async_computation.9 | async-start | bytes 2097152 | tf_op jit(solution)/shard_map/all_to_all | solution.py:60
  411.8 36.0 %all-to-all-done.6 = bf16[256,2,1024]{2,1,0:T(2,128)(2,1)} async-done(((bf16[256,2,1024]{2,1,0:T(2,128)(2,1)}), bf16[256,2,1024]{2,1,0:T(2,128)(2,1)}, u32[]{:S(2)}, u32[]{:S(2)}) %all-to-all-start.6) | async-done | bytes 1048608 | tf_op jit(solution)/shard_map/all_to_all | solution.py:60
  447.8 6.4 all-to-all-start.8
  455.1 6.4 reshape.742
  462.2 10.3 %psum.7 = f32[16,256]{1,0:T(8,128)S(1)} all-reduce(f32[16,256]{1,0:T(8,128)S(1)} %fusion.66), channel_id=1, replica_groups=mesh['z'=8,'yh'=2,'x'=4,'yl'=2,'c'=2] {'yl','c'}, use_global_device_ids=true, to_apply=%region_31.32 | all-reduce | flops 4096 | bytes 32768 | tf_op jit(solution)/shard_map/psum | solution.py:472
  473.6 15.2 %all-to-all-start.7 = ((bf16[256,4,256]{2,1,0:T(4,128)(2,1)}), bf16[256,4,256]{2,1,0:T(4,128)(2,1)S(1)}, u32[]{:S(2)}, u32[]{:S(2)}) async-start(bf16[256,4,256]{2,1,0:T(4,128)(2,1)} %broadcast_in_dim.75), calls=%async_computation.10 | async-start | bytes 1048576 | tf_op jit(solution)/shard_map/all_to_all | solution.py:60
  495.1 49.2 %reduce-scatter.8.cloned.1.call-done = bf16[128,2048]{1,0:T(8,128)(2,1)} async-done(((bf16[1024,2048]{1,0:T(8,128)(2,1)}), bf16[128,2048]{1,0:T(8,128)(2,1)}) %reduce-scatter.8.cloned.1.call-update) | async-done | bytes 524304 | tf_op jit(solution)/shard_map/reduce_scatter | solution.py:395
  546.9 6.7 %all-to-all-start.5 = ((bf16[16,16,3072]{2,1,0:T(8,128)(2,1)}), bf16[16,16,3072]{2,1,0:T(8,128)(2,1)}, u32[]{:S(2)}, u32[]{:S(2)}) async-start(bf16[16,16,3072]{2,1,0:T(8,128)(2,1)} %pad_maximum_fusion.1), calls=%async_computation.8 | async-start | bytes 3145728 | tf_op jit(solution)/shard_map/all_to_all | solution.py:60
  563.0 15.3 %all-to-all-done.5 = bf16[16,16,3072]{2,1,0:T(8,128)(2,1)} async-done(((bf16[16,16,3072]{2,1,0:T(8,128)(2,1)}), bf16[16,16,3072]{2,1,0:T(8,128)(2,1)}, u32[]{:S(2)}, u32[]{:S(2)}) %all-to-all-start.5) | async-done | bytes 1572896 | tf_op jit(solution)/shard_map/all_to_all | solution.py:60
  585.3 6.4 all-to-all-start.9
  595.6 9.1 %all_gather.19 = f32[8,16,1024]{2,1,0:T(8,128)S(1)} all-gather(f32[4,16,1024]{2,1,0:T(8,128)S(1)} %all_gather.18), channel_id=1, replica_groups=mesh['z'=8,'yh'=2,'x'=4,'yl'=2,'c'=2] {'yl'}, dimensions={0}, use_global_device_ids=true | all-gather | bytes 786432 | tf_op jit(solution)/shard_map/all_gather | solution.py:533
  620.5 5.4 shard_map.440
  (569 shorter events, 198.6 us)
Async XLA Ops:
  7.2 84.1 %copy-start = (bf16[4,4096]{1,0:T(4,128)(2,1)S(1)}, bf16[4,4096]{1,0:T(4,128)(2,1)}, u32[]{:S(2)}) copy-start(bf16[4,4096]{1,0:T(4,128)(2,1)} %param.25) | copy-start | bytes 98308
  7.2 100.5 %all-gather.4.cloned.1.call-start = ((), (), s32[]{:S(2)}) async-start(), calls=%async_computation.13 | async-start | bytes 4718592 | tf_op jit(solution)/shard_map/all_gather | solution.py:257
  40.7 139.6 %all-gather.6.cloned.1.call-start = ((), (), s32[]{:S(2)}) async-start(), calls=%async_computation.14 | async-start | bytes 4718592 | tf_op jit(solution)/shard_map/all_gather | solution.py:258
  41.8 191.0 %all-gather.8.cloned.1.call-start = ((), (), s32[]{:S(2)}) async-start(), calls=%async_computation.15 | async-start | bytes 4718592 | tf_op jit(solution)/shard_map/all_gather | solution.py:259
  52.6 30.3 %all-to-all-start = ((bf16[256,4,128]{2,1,0:T(4,128)(2,1)}), bf16[256,4,128]{2,1,0:T(4,128)(2,1)S(1)}, u32[]{:S(2)}, u32[]{:S(2)}) async-start(bf16[256,4,128]{2,1,0:T(4,128)(2,1)} %maximum_maximum_fusion), calls=%async_computation | async-start | bytes 524288 | tf_op jit(solution)/shard_map/all_to_all | solution.py:60
  85.2 24.2 %all-to-all-start.1 = ((f32[64,4,256]{2,1,0:T(4,128)}), f32[64,4,256]{2,1,0:T(4,128)S(1)}, u32[]{:S(2)}, u32[]{:S(2)}) async-start(f32[64,4,256]{2,1,0:T(4,128)} %copy.405), calls=%async_computation.1 | async-start | bytes 524288 | tf_op jit(solution)/shard_map/all_to_all | solution.py:60
  107.7 130.3 %collective-permute-start = (bf16[1024,2048]{1,0:T(8,128)(2,1)}, bf16[1024,2048]{1,0:T(8,128)(2,1)}, u32[]{:S(2)}, u32[]{:S(2)}) collective-permute-start(bf16[1024,2048]{1,0:T(8,128)(2,1)} %all-gather.4.cloned.1.call-done), channel_id=1, source_target_pairs={{0,1},{1,0},{2,3},{3,2},{4,5},{5,4},{6,7},{7,6},{8,9},{9,8},{10,11... | collective-permute-start | bytes 12582920 | tf_op jit(solution)/shard_map/ppermute | solution.py:64
  112.1 35.9 %all-to-all-start.2 = ((bf16[256,4,256]{2,1,0:T(4,128)(2,1)}), bf16[256,4,256]{2,1,0:T(4,128)(2,1)S(1)}, u32[]{:S(2)}, u32[]{:S(2)}) async-start(bf16[256,4,256]{2,1,0:T(4,128)(2,1)} %broadcast_in_dim.72), calls=%async_computation.2 | async-start | bytes 1048576 | tf_op jit(solution)/shard_map/all_to_all | solution.py:60
  125.5 49.5 %copy-start.86 = (f32[256]{0:T(256)}, f32[256]{0:T(256)S(1)}, u32[]{:S(2)}) copy-start(f32[256]{0:T(256)S(1)} %broadcast_multiply_fusion.8) | copy-start | bytes 3076
  125.7 49.5 %copy-start.90 = (f32[256]{0:T(256)}, f32[256]{0:T(256)S(1)}, u32[]{:S(2)}) copy-start(f32[256]{0:T(256)S(1)} %add_rsqrt_fusion.2) | copy-start | bytes 3076
  149.3 20.3 %all-to-all-start.3 = ((f32[256,1,32]{2,1,0:T(1,128)}), f32[256,1,32]{2,1,0:T(1,128)S(1)}, u32[]{:S(2)}, u32[]{:S(2)}) async-start(f32[256,1,32]{2,1,0:T(1,128)} %copy.407), calls=%async_computation.3 | async-start | bytes 262144 | tf_op jit(solution)/shard_map/all_to_all | solution.py:60
  155.7 335.5 %reduce-scatter.4.cloned.1.call-start = ((), (), s32[]{:S(2)}) async-start(), calls=%async_computation.16 | async-start | bytes 4718592 | tf_op jit(solution)/shard_map/reduce_scatter | solution.py:444
  180.3 75.3 %collective-permute-start.1 = (bf16[1024,2048]{1,0:T(8,128)(2,1)}, bf16[1024,2048]{1,0:T(8,128)(2,1)}, u32[]{:S(2)}, u32[]{:S(2)}) collective-permute-start(bf16[1024,2048]{1,0:T(8,128)(2,1)} %all-gather.6.cloned.1.call-done), channel_id=1, source_target_pairs={{0,1},{1,0},{2,3},{3,2},{4,5},{5,4},{6,7},{7,6},{8,9},{9,8},{10,11... | collective-permute-start | bytes 12582920 | tf_op jit(solution)/shard_map/ppermute | solution.py:64
  182.9 52.3 %copy-start.68 = (f32[1024]{0:T(1024)S(1)}, f32[1024]{0:T(1024)}, u32[]{:S(2)}) copy-start(f32[1024]{0:T(1024)} %get-tuple-element.252) | copy-start | bytes 12292
  232.8 28.6 %collective-permute-start.2 = (bf16[1024,2048]{1,0:T(8,128)(2,1)}, bf16[1024,2048]{1,0:T(8,128)(2,1)}, u32[]{:S(2)}, u32[]{:S(2)}) collective-permute-start(bf16[1024,2048]{1,0:T(8,128)(2,1)} %all-gather.8.cloned.1.call-done), channel_id=1, source_target_pairs={{0,1},{1,0},{2,3},{3,2},{4,5},{5,4},{6,7},{7,6},{8,9},{9,8},{10,11... | collective-permute-start | bytes 12582920 | tf_op jit(solution)/shard_map/ppermute | solution.py:64
  285.5 84.0 %copy-start.63 = (f32[1024]{0:T(1024)}, f32[1024]{0:T(1024)S(1)}, u32[]{:S(2)}) copy-start(f32[1024]{0:T(1024)S(1)} %get-tuple-element.246) | copy-start | bytes 12292
  314.0 21.0 %collective-permute-start.3 = (bf16[1024,2048]{1,0:T(8,128)(2,1)}, bf16[1024,2048]{1,0:T(8,128)(2,1)}, u32[]{:S(2)}, u32[]{:S(2)}) collective-permute-start(bf16[1024,2048]{1,0:T(8,128)(2,1)} %pad_maximum_fusion), channel_id=1, source_target_pairs={{0,1},{1,0},{2,3},{3,2},{4,5},{5,4},{6,7},{7,6},{8,9},{9,8},{10,11... | collective-permute-start | bytes 12582920 | tf_op jit(solution)/shard_map/ppermute | solution.py:64
  339.3 155.8 %reduce-scatter.6.cloned.1.call-start = ((), (), s32[]{:S(2)}) async-start(), calls=%async_computation.17 | async-start | bytes 4718592 | tf_op jit(solution)/shard_map/reduce_scatter | solution.py:407
  342.9 7.4 %collective-permute-start.4 = (bf16[1024,2048]{1,0:T(8,128)(2,1)S(1)}, bf16[1024,2048]{1,0:T(8,128)(2,1)S(1)}, u32[]{:S(2)}, u32[]{:S(2)}) collective-permute-start(bf16[1024,2048]{1,0:T(8,128)(2,1)S(1)} %convolution_convert_fusion.3), channel_id=1, source_target_pairs={{0,1},{1,0},{2,3},{3,2},{4,5},{5,4},{6,7},{7,6},{8,9},{9,8},{10,11... | collective-permute-start | bytes 12582920 | tf_op jit(solution)/shard_map/ppermute | solution.py:64
  353.5 190.8 %reduce-scatter.8.cloned.1.call-start = ((), (), s32[]{:S(2)}) async-start(), calls=%async_computation.18 | async-start | bytes 4718592 | tf_op jit(solution)/shard_map/reduce_scatter | solution.py:395
  357.7 7.4 %collective-permute-start.5 = (bf16[1024,2048]{1,0:T(8,128)(2,1)S(1)}, bf16[1024,2048]{1,0:T(8,128)(2,1)S(1)}, u32[]{:S(2)}, u32[]{:S(2)}) collective-permute-start(bf16[1024,2048]{1,0:T(8,128)(2,1)S(1)} %convolution_convert_fusion.2), channel_id=1, source_target_pairs={{0,1},{1,0},{2,3},{3,2},{4,5},{5,4},{6,7},{7,6},{8,9},{9,8},{10,11... | collective-permute-start | bytes 12582920 | tf_op jit(solution)/shard_map/ppermute | solution.py:64
  396.2 51.5 %all-to-all-start.6 = ((bf16[256,2,1024]{2,1,0:T(2,128)(2,1)}), bf16[256,2,1024]{2,1,0:T(2,128)(2,1)}, u32[]{:S(2)}, u32[]{:S(2)}) async-start(bf16[256,2,1024]{2,1,0:T(2,128)(2,1)} %reshape.741), calls=%async_computation.9 | async-start | bytes 2097152 | tf_op jit(solution)/shard_map/all_to_all | solution.py:60
  447.8 24.9 %all-to-all-start.8 = ((f32[256,1,256]{2,1,0:T(1,128)}), f32[256,1,256]{2,1,0:T(1,128)S(1)}, u32[]{:S(2)}, u32[]{:S(2)}) async-start(f32[256,1,256]{2,1,0:T(1,128)} %reshape.743), calls=%async_computation.11 | async-start | bytes 524288 | tf_op jit(solution)/shard_map/all_to_all | solution.py:60
  473.6 73.3 %all-to-all-start.7 = ((bf16[256,4,256]{2,1,0:T(4,128)(2,1)}), bf16[256,4,256]{2,1,0:T(4,128)(2,1)S(1)}, u32[]{:S(2)}, u32[]{:S(2)}) async-start(bf16[256,4,256]{2,1,0:T(4,128)(2,1)} %broadcast_in_dim.75), calls=%async_computation.10 | async-start | bytes 1048576 | tf_op jit(solution)/shard_map/all_to_all | solution.py:60
  546.9 31.4 %all-to-all-start.5 = ((bf16[16,16,3072]{2,1,0:T(8,128)(2,1)}), bf16[16,16,3072]{2,1,0:T(8,128)(2,1)}, u32[]{:S(2)}, u32[]{:S(2)}) async-start(bf16[16,16,3072]{2,1,0:T(8,128)(2,1)} %pad_maximum_fusion.1), calls=%async_computation.8 | async-start | bytes 3145728 | tf_op jit(solution)/shard_map/all_to_all | solution.py:60
  563.0 45.7 %copy-start.52 = (f32[16,1280]{1,0:T(8,128)S(1)}, f32[16,1280]{1,0:T(8,128)}, u32[]{:S(2)}) copy-start(f32[16,1280]{1,0:T(8,128)} %param.36) | copy-start | bytes 245764
  563.0 45.9 %copy-start.51 = (f32[4,16,512]{2,1,0:T(8,128)S(1)}, f32[4,16,512]{2,1,0:T(8,128)}, u32[]{:S(2)}) copy-start(f32[4,16,512]{2,1,0:T(8,128)} %param.30) | copy-start | bytes 393220
  585.3 20.7 %all-to-all-start.9 = ((f32[256,1,128]{2,1,0:T(1,128)}), f32[256,1,128]{2,1,0:T(1,128)S(1)}, u32[]{:S(2)}, u32[]{:S(2)}) async-start(f32[256,1,128]{2,1,0:T(1,128)} %broadcast_in_dim.83), calls=%async_computation.12 | async-start | bytes 262144 | tf_op jit(solution)/shard_map/all_to_all | solution.py:60
  604.9 4.1 collective-permute-start.6
  606.0 5.1 collective-permute-start.8
  609.3 7.8 %collective-permute-start.7 = (f32[4,16,16]{2,1,0:T(8,128)S(1)}, f32[4,16,16]{2,1,0:T(8,128)S(1)}, u32[]{:S(2)}, u32[]{:S(2)}) collective-permute-start(f32[4,16,16]{2,1,0:T(8,128)S(1)} %fusion.196), channel_id=1, source_target_pairs={{0,2},{2,0},{1,3},{3,1},{4,6},{6,4},{5,7},{7,5},{8,10},{10,8},{9,1... | collective-permute-start | bytes 12296 | tf_op jit(solution)/shard_map/ppermute | solution.py:64
  615.5 1.9 collective-permute-start.9
  (118 other events, 932.2 us)
Sparse Core Ops, SparseCore 0:
  40.8 66.8 all-gather.3
  110.0 67.4 all-gather.5
  179.4 53.4 all-gather.7
  339.5 53.7 reduce-scatter.3
  395.7 82.0 reduce-scatter.5
  480.1 64.1 reduce-scatter.7
where the time goes:
time: 654 us; the launch traced here: 643 us
  waiting for transfers between devices  230 us (35%)
  matrix products  119 us (18%)
  starting transfers between devices  88.2 us (13%)
  local copies, waits for them, and re-layouts  75.7 us (12%)
  blocking collectives  52.3 us (8%)
  other arithmetic  41.6 us (6%)
  between operations  30.2 us (5%)
    all_to_all x9, waiting for transfers between devices, exchange(): return lax.all_to_all(v, axes, 0, 0, tiled=True)  104 us
    dot_general x46, matrix products, dot(): lax.dot_general(lhs, rhs, (((lhs_dim,), (rhs_dim,)), ((), ())), precision...  82.5 us
    all_to_all x9, starting transfers between devices, exchange(): return lax.all_to_all(v, axes, 0, 0, tiled=True)  80.5 us
    reduce_scatter x1, waiting for transfers between devices, on_device(): lax.psum_scatter(second_sum, 'z', scatter_dimension=0, tiled=True)  49.2 us
    all_gather x1, waiting for transfers between devices, on_device(): second_mine = lax.all_gather(second_z, 'z', axis=0, tiled=True)  48.1 us
    all_to_all x1, blocking collectives, exchange(): return lax.all_to_all(v, axes, 0, 0, tiled=True)  29 us
    unnamed x266, local copies, waits for them, and re-layouts  23.2 us
    all_gather x1, waiting for transfers between devices, on_device(): attn_mine = lax.all_gather(attn_z, 'z', axis=0, tiled=True)  14.6 us
  transfers between devices with their start and end apart: 25, of which 11 were waited for; matrix products, arithmetic and copies ran while one was open for 23% of the time, Pallas kernels for 0%

commit v1 on v0

--- a/solution.py
+++ b/solution.py
@@ -57,11 +57,78 @@
 
 
 def exchange(v, axes):
-    return lax.all_to_all(v, axes, 0, 0, tiled=True)
+    return lax.all_to_all(v, axes, 0, 0)
+
+
+def to_all(v, axes):
+    return exchange(jnp.broadcast_to(v[None], (lax.axis_size(axes),) + v.shape), axes)
+
+
+def after(v, *others):
+    return lax.optimization_barrier((v,) + others)[0]
 
 
 def swap(v, axis):
     return lax.ppermute(v, axis, [(0, 1), (1, 0)])
+
+
+def shift(v, axes, by):
+    size = lax.axis_size(axes)
+    return lax.ppermute(v, axes, [(i, (i + by) % size) for i in range(size)])
+
+
+def gather_first(v, axes):
+    if lax.axis_size(axes) == 2:
+        return (shift(v, axes, 1),)
+    return shift(v, axes, 1), shift(v, axes, -1)
+
+
+def gather_rest(v, axes, got):
+    if lax.axis_size(axes) == 2:
+        return (v,) + got
+    before, next_ = got
+    cut = v.shape[0] // 2
+    across = jnp.concatenate([shift(before[:cut], axes, 1), shift(next_[cut:], axes, -1)], axis=0)
+    return v, next_, across, before
+
+
+def all_after(values, *others):
+    return lax.optimization_barrier(tuple(values) + others)[: len(values)]
+
+
+def reduce_first(piece, axes):
+    if lax.axis_size(axes) == 2:
+        return ()
+    across = piece(2)
+    cut = across.shape[0] // 2
+    return shift(across[:cut], axes, 1), shift(across[cut:], axes, -1)
+
+
+def reduce_rest(piece, axes, got):
+    if lax.axis_size(axes) == 2:
+        return piece(0).astype(F32) + shift(piece(1), axes, 1).astype(F32)
+    from_before, from_after = got
+    cut = from_before.shape[0]
+    up, down = piece(1), piece(3)
+    up = jnp.concatenate([added(up[:cut], from_before), up[cut:]], axis=0)
+    down = jnp.concatenate([down[:cut], added(down[cut:], from_after)], axis=0)
+    from_before = shift(up, axes, 1).astype(F32)
+    from_after = shift(down, axes, -1).astype(F32)
+    return piece(0).astype(F32) + from_before + from_after
+
+
+def added(one, two):
+    return (one.astype(F32) + two.astype(F32)).astype(BF)
+
+
+def placed(blocks, index, size, axis):
+    shape = list(blocks[0].shape)
+    shape[axis] *= size
+    out = jnp.zeros(shape, blocks[0].dtype)
+    for r, block in enumerate(blocks):
+        where = lax.rem(index + r, size) * blocks[0].shape[axis]
+        out = lax.dynamic_update_slice_in_dim(out, block, where, axis)
+    return out
 
 
 def in_order(index, mine, other, axis):
@@ -69,6 +136,44 @@
         index == 0,
         jnp.concatenate([mine, other], axis=axis),
         jnp.concatenate([other, mine], axis=axis),
+    )
+
+
+def place_y(blocks, y_at):
+    first, _, rows, cols = blocks[0].shape
+    out = jnp.zeros((first, 2, rows, 2 * cols), blocks[0].dtype)
+    for r, block in enumerate(blocks):
+        where = lax.rem(y_at + r, 4)
+        out = lax.dynamic_update_slice(out, block, (0, where // 2, 0, where % 2 * cols))
+    return out
+
+
+def join_y(low, high):
+    cut = 3 * low.shape[-1] // 4
+    return jnp.concatenate(
+        [low[..., :cut], high[..., :cut], low[..., cut:], high[..., cut:]], axis=-1
+    )
+
+
+def split_y(v, side):
+    width = v.shape[-1] // 8
+    return jnp.concatenate(
+        [
+            v[..., 3 * side * width : 3 * (side + 1) * width],
+            v[..., (6 + side) * width : (7 + side) * width],
+        ],
+        axis=-1,
+    )
+
+
+def gather_direct(v, axes):
+    return [v] + [shift(v, axes, -by) for by in range(1, lax.axis_size(axes))]
+
+
+def in_ring_order(blocks, index):
+    size = len(blocks)
+    return lax.dynamic_slice_in_dim(
+        jnp.concatenate(blocks + blocks, axis=0), lax.rem(size - index, size), size, axis=0
     )
 
 
@@ -160,40 +265,88 @@
     return (new_weight, first_new, second_new)
 
 
-def heads_of(v):
-    return v.reshape(SEQ, -1, HDIM)
-
-
-def raw_scores(q_low, k_low):
-    return jnp.einsum(
-        "qhd,khd->hqk", heads_of(q_low), heads_of(k_low), preferred_element_type=F32
-    ) * (1.0 / math.sqrt(HDIM))
-
-
-def attend(q_low, k_low, v_low):
-    scores = raw_scores(q_low, k_low)
-    peak = jnp.max(scores, axis=-1, keepdims=True)
-    log_total = peak + jnp.log(jnp.sum(jnp.exp(scores - peak), axis=-1, keepdims=True))
-    probs = jnp.exp(scores - log_total).astype(BF)
-    out = jnp.einsum("hqk,khd->qhd", probs, heads_of(v_low), preferred_element_type=F32)
-    return out.reshape(q_low.shape).astype(BF), log_total
-
-
-def attend_back(q_low, k_low, v_low, log_total, d_att):
-    shape = q_low.shape
-    probs = jnp.exp(raw_scores(q_low, k_low) - log_total)
-    d_heads = heads_of(d_att)
-    d_probs = jnp.einsum("qhd,khd->hqk", d_heads, heads_of(v_low), preferred_element_type=F32)
-    d_value = jnp.einsum("hqk,qhd->khd", probs.astype(BF), d_heads, preferred_element_type=F32)
-    row_dot = jnp.sum(d_probs * probs, axis=-1, keepdims=True)
-    d_raw = (probs * (d_probs - row_dot) * (1.0 / math.sqrt(HDIM))).astype(BF)
-    d_query = jnp.einsum("hqk,khd->qhd", d_raw, heads_of(k_low), preferred_element_type=F32)
-    d_key = jnp.einsum("hqk,qhd->khd", d_raw, heads_of(q_low), preferred_element_type=F32)
-    return (
-        d_query.reshape(shape).astype(BF),
-        d_key.reshape(shape).astype(BF),
-        d_value.reshape(shape).astype(BF),
-    )
+def across_rows(lhs, rhs):
+    return dot(lhs, rhs, 1, 1)
+
+
+def head_probs(q, k, side):
+    lane = lax.broadcasted_iota(jnp.int32, (1, 2 * HDIM), 1)
+    mask = (lane // HDIM == side).astype(F32)
+    scores = across_rows((q.astype(F32) * mask).astype(BF), k) * (1.0 / math.sqrt(HDIM))
+    grown = jnp.exp(scores - jnp.max(scores, axis=-1, keepdims=True))
+    return grown / jnp.sum(grown, axis=-1, keepdims=True), mask
+
+
+def attend_kernel(*refs):
+    for half in range(2):
+        q, k, v = (r[...] for r in refs[3 * half : 3 * half + 3])
+        out = 0.0
+        for side in range(2):
+            probs, mask = head_probs(q, k, side)
+            out = out + mask * dot(probs.astype(BF), v, 1, 0)
+        refs[6 + half][...] = out.astype(BF)
+
+
+def attend_back_kernel(*refs):
+    block = pl.program_id(0)
+    per = pl.num_programs(0) // 2
+    for half in range(2):
+        q, k, v, d_att = (r[...] for r in refs[4 * half : 4 * half + 4])
+        d_q, d_k, d_v = 0.0, 0.0, 0.0
+        for side in range(2):
+            probs, mask = head_probs(q, k, side)
+            d_probs = across_rows((d_att.astype(F32) * mask).astype(BF), v)
+            d_v = d_v + mask * dot(probs.astype(BF), d_att, 0, 0)
+            row_dot = jnp.sum(d_probs * probs, axis=-1, keepdims=True)
+            d_raw = (probs * (d_probs - row_dot) * (1.0 / math.sqrt(HDIM))).astype(BF)
+            d_q = d_q + mask * dot(d_raw, k, 1, 0)
+            d_k = d_k + mask * dot(d_raw, q, 0, 0)
+        for at, value in enumerate((d_q, d_k, d_v)):
+            where = pl.multiple_of(qkv_block(block, at, per) * 2 * HDIM, 2 * HDIM)
+            refs[8 + half][:, pl.ds(where, 2 * HDIM)] = value.astype(BF)
+
+
+def qkv_block(j, at, per):
+    return (j // per) * 3 * per + at * per + j % per
+
+
+def columns(at=None, per=1):
+    if at is None:
+        return pl.BlockSpec((SEQ, 2 * HDIM), lambda j: (0, j))
+    return pl.BlockSpec((SEQ, 2 * HDIM), lambda j: (0, qkv_block(j, at, per)))
+
+
+def attend(qkv):
+    width = qkv[0].shape[1] // 3
+    groups = width // (2 * HDIM)
+    return pl.pallas_call(
+        attend_kernel,
+        grid=(groups,),
+        in_specs=[columns(at, groups // 2) for at in range(3)] * 2,
+        out_specs=[columns()] * 2,
+        out_shape=[jax.ShapeDtypeStruct((SEQ, width), BF)] * 2,
+        cost_estimate=pl.CostEstimate(
+            flops=16 * SEQ * SEQ * width, bytes_accessed=16 * SEQ * width, transcendentals=8 * SEQ * SEQ
+        ),
+        interpret=INTERPRET,
+    )(*(qkv[0],) * 3, *(qkv[1],) * 3)
+
+
+def attend_back(qkv, d_att):
+    width = qkv[0].shape[1] // 3
+    groups = width // (2 * HDIM)
+    whole = pl.BlockSpec((SEQ, 3 * width), lambda j: (0, 0))
+    return pl.pallas_call(
+        attend_back_kernel,
+        grid=(groups,),
+        in_specs=([columns(at, groups // 2) for at in range(3)] + [columns()]) * 2,
+        out_specs=[whole] * 2,
+        out_shape=[jax.ShapeDtypeStruct((SEQ, 3 * width), BF)] * 2,
+        cost_estimate=pl.CostEstimate(
+            flops=40 * SEQ * SEQ * width, bytes_accessed=28 * SEQ * width, transcendentals=8 * SEQ * SEQ
+        ),
+        interpret=INTERPRET,
+    )(*(qkv[0],) * 3, d_att[0], *(qkv[1],) * 3, d_att[1])
 
 
 def on_device(
@@ -224,7 +377,6 @@
 ):
     n_shard = lax.axis_size(SHARD)
     n_all = lax.axis_size(ALL)
-    n_plane = lax.axis_size(PLANE)
     count_all = n_all * SEQ * PATCH
     yl, core = lax.axis_index("yl"), lax.axis_index("c")
     sub = 2 * yl + core
@@ -233,33 +385,26 @@
     quarter = D // 4
     wide = 4 * half
 
+    n_z, n_x = lax.axis_size("z"), lax.axis_size("x")
+    x_at = lax.axis_index("x")
+    yh = lax.axis_index("yh")
+    y_at = 2 * yh + yl
     attn_low = lax.dynamic_slice_in_dim(attn_w, core * quarter, quarter, axis=2).astype(BF)
-    mlp_low = lax.dynamic_slice_in_dim(mlp_w, yl * 4, 4, axis=0).astype(BF)
-    own_rows = jnp.concatenate(
-        [
-            attn_low.transpose(1, 0, 2).reshape(RB, 4 * quarter),
-            mlp_low.transpose(1, 0, 2).reshape(RB, wide),
-        ],
-        axis=1,
-    )
-    plane_rows = exchange(
-        jnp.broadcast_to(own_rows[None], (n_plane,) + own_rows.shape), PLANE
-    ).reshape(n_plane // 2, 2, RB, -1)
-    z_rows = n_plane // 2 * RB
-    attn_z = (
-        plane_rows[..., : 4 * quarter]
-        .reshape(n_plane // 2, 2, RB, 4, quarter)
-        .transpose(0, 2, 3, 1, 4)
-        .reshape(z_rows, wide)
-    )
-    first_z = plane_rows[:, 0, :, 4 * quarter :].reshape(z_rows, wide)
-    second_z = plane_rows[:, 1, :, 4 * quarter :].reshape(z_rows, wide)
-    attn_mine = lax.all_gather(attn_z, "z", axis=0, tiled=True)
-    first_mine = lax.all_gather(first_z, "z", axis=0, tiled=True)
-    second_mine = lax.all_gather(second_z, "z", axis=0, tiled=True)
-    attn_halves = (attn_mine, swap(attn_mine, "c"))
-    first_halves = (first_mine, swap(first_mine, "c"))
-    second_halves = (second_mine, swap(second_mine, "c"))
+    attn_own = attn_low.transpose(1, 0, 2).reshape(RB, 4 * quarter)
+    mlp_low = (
+        lax.dynamic_slice_in_dim(mlp_w.reshape(2, 4, RB, half), 2 * yl, 2, axis=1)
+        .astype(BF)
+        .transpose(0, 2, 1, 3)
+        .reshape(2, RB, D)
+    )
+    z_at = lax.axis_index("z")
+    second_x = in_ring_order(gather_direct(mlp_low[1][None], "x"), x_at)
+    second_parts = gather_direct(second_x.reshape(1, 1, n_x * RB, D), ("yh", "yl"))
+    second_y = place_y(second_parts, y_at).reshape(2 * n_x * RB, wide)
+    second_mine = lax.all_gather(second_y, "z", axis=0, tiled=True)
+    both_z = in_ring_order(
+        gather_direct(jnp.concatenate([attn_own, mlp_low[0]], axis=1)[None], "z"), z_at
+    )
 
     label_own = lax.dynamic_index_in_dim(labels, sub, keepdims=False)
     time_own = lax.dynamic_index_in_dim(timesteps, sub, keepdims=False)
@@ -294,6 +439,20 @@
         axis=2,
     )
     got = exchange(sent, ALL)
+    attn_own, first_own = both_z[..., :D], both_z[:, None, :, D:]
+    attn_got = gather_first(attn_own, ("yh", "yl"))
+    first_got = gather_first(first_own, "x")
+    low_y = yl == 0
+    own, next_, across, before = gather_rest(attn_own, ("yh", "yl"), attn_got)
+    pair_own = join_y(jnp.where(low_y, own, before), jnp.where(low_y, next_, own))
+    pair_far = join_y(jnp.where(low_y, across, next_), jnp.where(low_y, before, across))
+    attn_y = in_order(yh, pair_own[:, None], pair_far[:, None], 1).reshape(2 * n_z, 1, RB, wide)
+    first_x = placed(gather_rest(first_own, "x", first_got), x_at, n_x, 1).reshape(
+        n_z, 1, n_x * RB, D
+    )
+    attn_y, first_x = all_after((attn_y, first_x), got)
+    attn_got = gather_first(attn_y, "x")
+    first_got = gather_first(first_x, ("yh", "yl"))
     marks = got[:, 0, lanes_int : lanes_int + 4].astype(F32)
     labels_all = (marks[:, 0] * 32.0 + marks[:, 1]).astype(jnp.int32)
     times_all = marks[:, 2] * 32.0 + marks[:, 3]
@@ -317,47 +476,50 @@
         temb_low[:, FREQ:].reshape(RB, n_shard, 4, vec_cols), sub, 1, axis=2
     ).reshape(RB, n_shard * vec_cols)
     cond_parts = dot(temb_cols, hid_t, 0, 0)
-    cond_parts = exchange(cond_parts.reshape(n_shard, vec_cols, n_all), SHARD)
+    cond_parts = exchange(
+        after(cond_parts.reshape(n_shard, vec_cols, n_all), second_x), SHARD
+    )
     onehot = (labels_all[:, None] == jnp.arange(NCLS)[None, :]).astype(BF)
     label_rows = dot(label_table.astype(BF), onehot, 0, 1)
     cond_t = jnp.sum(cond_parts, axis=0) + label_rows + rounded(vec_w[2])[:, None]
     act_own = jax.nn.silu(cond_t).astype(BF)
-    act_t = exchange(jnp.broadcast_to(act_own[None], (n_all,) + act_own.shape), ALL).reshape(
-        D, n_all
-    )
+    act_t = to_all(after(act_own, second_y), ALL)
+    attn_mine = placed(gather_rest(attn_y, "x", attn_got), x_at, n_x, 1).reshape(D, wide)
+    first_mine = place_y(gather_rest(first_x, ("yh", "yl"), first_got), y_at).reshape(D, wide)
+    patch_vals = lax.dynamic_index_in_dim(noisy_patches, sub, keepdims=False).reshape(SEQ, PATCH)
+    x_in = dot(patch_vals, io_low[:PATCH], 1, 0) + vec_f[0] + grid_table()
+    norm_one, inv_one = layer_norm(x_in)
+    act_t, attn_mine, first_mine, norm_one = lax.optimization_barrier(
+        (act_t, attn_mine, first_mine, norm_one)
+    )
+    act_t = act_t.reshape(D, n_all)
     mods_sent = dot(act_t, mod_col, 0, 0) + own_mod_bias.T.reshape(1, 2 * RB)
     mods = (
-        exchange(mods_sent, ALL)
-        .reshape(n_shard, 8, RB)
-        .transpose(1, 0, 2)
-        .reshape(8, 1, D)
-    )
-
-    patch_vals = lax.dynamic_index_in_dim(noisy_patches, sub, keepdims=False).reshape(SEQ, PATCH)
+        exchange(mods_sent[:, None], ALL).reshape(n_shard, 8, RB).transpose(1, 0, 2).reshape(8, 1, D)
+    )
+    second_mine = after(second_mine, mods)
+    attn_halves = (attn_mine, swap(attn_mine, "c"))
+    first_halves = (first_mine, swap(first_mine, "c"))
+    second_halves = (second_mine, swap(second_mine, "c"))
+
     target = lax.dynamic_index_in_dim(true_noise, sub, keepdims=False).reshape(SEQ, PATCH)
     head_low = rounded(head_b)
-    x_in = dot(patch_vals, io_low[:PATCH], 1, 0) + vec_f[0] + grid_table()
-    norm_one, inv_one = layer_norm(x_in)
     h_one = (norm_one * (1.0 + mods[1]) + mods[0]).astype(BF)
     own_half = (core, 1 - core)
 
     def attn_bias(row, which):
         rows = vec_f[row].reshape(2, 2, quarter)
-        return lax.dynamic_index_in_dim(rows, which, axis=1, keepdims=False).reshape(half)
+        return lax.dynamic_index_in_dim(rows, which, axis=1, keepdims=False)
 
     qkv = []
-    attended = []
-    log_totals = []
+    for weight, which in zip(attn_halves, own_half):
+        bias = jnp.stack(
+            [attn_bias(11, which), jnp.zeros((2, quarter), F32), attn_bias(12, which)], axis=1
+        )
+        qkv.append((dot(h_one, weight[:, : 3 * half], 1, 0) + bias.reshape(3 * half)).astype(BF))
+    attended = attend(qkv)
     attn_out = vec_f[13]
-    for weight, which in zip(attn_halves, own_half):
-        proj = dot(h_one, weight[:, : 3 * half], 1, 0)
-        q_low = (proj[:, :half] + attn_bias(11, which)).astype(BF)
-        k_low = proj[:, half : 2 * half].astype(BF)
-        v_low = (proj[:, 2 * half :] + attn_bias(12, which)).astype(BF)
-        att, log_total = attend(q_low, k_low, v_low)
-        qkv.append((q_low, k_low, v_low))
-        attended.append(att)
-        log_totals.append(log_total)
+    for weight, att in zip(attn_halves, attended):
         attn_out = attn_out + dot(att, weight[:, 3 * half :], 1, 1)
     x_one = x_in + mods[2] * attn_out
     norm_two, inv_two = layer_norm(x_one)
@@ -390,58 +552,73 @@
     d_mlp = mods[5] * d_two
     d_mlp_low = d_mlp.astype(BF)
     grad_bfc = jnp.sum(d_mlp, axis=0)
-    grad_second = [dot(d_mlp_low, act, 0, 0).astype(BF) for act in act_mlp]
-    second_sum = chip_sum(grad_second)
-    second_z = lax.psum_scatter(second_sum, "z", scatter_dimension=0, tiled=True)
+    second_sum = chip_sum([dot(d_mlp_low, act, 0, 0).astype(BF) for act in act_mlp])
+    second_z = lax.psum_scatter(second_sum, "z", scatter_dimension=0, tiled=True).reshape(
+        2 * n_x, RB, wide
+    )
     d_pre_low = []
     hid_bias = []
     d_h_two = 0.0
-    for pre, first, second in zip(pre_mlp, first_halves, second_halves):
-        d_act = dot(d_mlp_low, second, 1, 0)
+    d_acts = [dot(d_mlp_low, second, 1, 0) for second in second_halves]
+    d_acts = lax.optimization_barrier(tuple(d_acts) + (second_sum,))[:2]
+    for pre, first, d_act in zip(pre_mlp, first_halves, d_acts):
         d_pre = jax.vjp(gelu_tanh, pre)[1](d_act)[0]
         hid_bias.append(jnp.sum(d_pre, axis=0).reshape(4, half))
         d_pre_low.append(d_pre.astype(BF))
         d_h_two = d_h_two + dot(d_pre_low[-1], first, 1, 1)
-    grad_first = [dot(h_two, d, 0, 0).astype(BF) for d in d_pre_low]
-    first_sum = chip_sum(grad_first)
-    first_z = lax.psum_scatter(first_sum, "z", scatter_dimension=0, tiled=True)
+    first_sum = chip_sum([dot(h_two, d, 0, 0).astype(BF) for d in d_pre_low])
+    first_parts = first_sum.reshape(n_z, 2, n_x * RB, wide)
+
+    def first_piece(r):
+        where = lax.rem(y_at + r, 4)
+        return lax.dynamic_slice(
+            first_parts, (0, where // 2, 0, where % 2 * D), (n_z, 1, n_x * RB, D)
+        )
+
+    first_step = reduce_first(first_piece, ("yh", "yl"))
     grad_bhid = in_order(core, hid_bias[0], hid_bias[1], 1)
     d_shift_two = jnp.sum(d_h_two, axis=0)
     d_scale_two = jnp.sum(d_h_two * norm_two, axis=0)
     d_one = d_two + norm_back(d_h_two * (1.0 + mods[4]), norm_two, inv_two)
     d_gate_one = jnp.sum(d_one * attn_out, axis=0)
     d_attn = mods[2] * d_one
-    d_attn_low = d_attn.astype(BF)
+    d_attn_low = after(d_attn.astype(BF), first_sum)
     grad_bout = jnp.sum(d_attn, axis=0)
-    grad_attn = []
-    qv_bias = []
-    d_h_one = 0.0
-    for weight, (q_low, k_low, v_low), att, log_total in zip(
-        attn_halves, qkv, attended, log_totals
-    ):
-        d_att = dot(d_attn_low, weight[:, 3 * half :], 1, 0).astype(BF)
-        d_query, d_key, d_value = attend_back(q_low, k_low, v_low, log_total, d_att)
-        d_proj = jnp.concatenate([d_query, d_key, d_value], axis=1)
-        grad_attn.append(
+    d_att = [dot(d_attn_low, weight[:, 3 * half :], 1, 0).astype(BF) for weight in attn_halves]
+    d_proj = attend_back(qkv, lax.optimization_barrier(tuple(d_att) + tuple(first_step))[:2])
+    first_y = reduce_rest(first_piece, ("yh", "yl"), first_step).astype(BF)
+    attn_sum = chip_sum(
+        [
             jnp.concatenate(
-                [
-                    dot(h_one, d_proj, 0, 0).astype(BF),
-                    dot(d_attn_low, att, 0, 0).astype(BF),
-                ],
-                axis=1,
+                [dot(h_one, d, 0, 0).astype(BF), dot(d_attn_low, att, 0, 0).astype(BF)], axis=1
             )
-        )
-        qv_bias.append(
-            jnp.stack(
-                [
-                    jnp.sum(d_query.astype(F32), axis=0),
-                    jnp.sum(d_value.astype(F32), axis=0),
-                ]
-            ).reshape(2, 2, 1, quarter)
-        )
-        d_h_one = d_h_one + dot(d_proj, weight[:, : 3 * half], 1, 1)
-    attn_sum = chip_sum(grad_attn)
-    attn_zg = lax.psum_scatter(attn_sum, "z", scatter_dimension=0, tiled=True)
+            for d, att in zip(d_proj, attended)
+        ]
+    )
+    attn_parts = attn_sum.reshape(2 * n_z, n_x, RB, wide)
+
+    def attn_piece(r):
+        return lax.dynamic_slice_in_dim(attn_parts, lax.rem(x_at + r, n_x), 1, axis=1)
+
+    attn_step = reduce_first(attn_piece, "x")
+    d_h_one = sum(
+        dot(d, weight[:, : 3 * half], 1, 1) for d, weight in zip(d_proj, attn_halves)
+    )
+    first_back = exchange(
+        after(first_y.reshape(n_z * n_x, RB, D), attn_sum), ("z", "x")
+    )
+    second_back = exchange(
+        jnp.stack([second_z[..., :D], second_z[..., D:]], axis=1).reshape(4 * n_x, RB, D), PLANE
+    )
+    qv_bias = [
+        jnp.sum(d.astype(F32), axis=0).reshape(2, 3, quarter)[:, ::2].transpose(1, 0, 2)[:, :, None]
+        for d in d_proj
+    ]
+    attn_x = reduce_rest(attn_piece, "x", attn_step).astype(BF).reshape(2 * n_z, RB, wide)
+    attn_back = exchange(
+        jnp.stack([split_y(attn_x, 0), split_y(attn_x, 1)], axis=1).reshape(4 * n_z, RB, D),
+        ("z", "yh", "yl"),
+    )
     grad_bqv = in_order(core, qv_bias[0], qv_bias[1], 2).reshape(2, D)
     d_shift_one = jnp.sum(d_h_one, axis=0)
     d_scale_one = jnp.sum(d_h_one * norm_one, axis=0)
@@ -461,23 +638,25 @@
         ]
     )
 
+    lanes = 128
+    tiles = 2 * D // lanes
     dmod_sent = jnp.broadcast_to(
-        d_mods.astype(BF).reshape(1, 4, 2 * D), (n_shard, 4, 2 * D)
-    ).reshape(n_all, 2 * D)
+        d_mods.astype(BF).reshape(1, 4, tiles, lanes), (n_shard, 4, tiles, lanes)
+    ).reshape(n_all, tiles, lanes)
     dmod_all = exchange(dmod_sent, ALL)
     mod_sub = lax.dynamic_slice_in_dim(mod_own, 2 * sub, 2, axis=0)
     act_rows = lax.dynamic_slice_in_dim(act_t, shard * RB, RB, axis=0)
+    dmod_all = dmod_all.reshape(n_all, 2 * D)
     grad_mod = dot(act_rows, dmod_all, 1, 0).reshape(RB, 2, D).transpose(1, 0, 2)
     d_act = dot(mod_sub.transpose(1, 0, 2).reshape(RB, 2 * D), dmod_all, 1, 1)
-    d_act = lax.psum(d_act, ("yl", "c"))
+    d_act = d_act + swap(d_act, "c")
+    d_act = d_act + swap(d_act, "yl")
     d_act = lax.dynamic_slice_in_dim(d_act, sub * vec_cols, vec_cols, axis=0)
     d_cond = jax.vjp(jax.nn.silu, cond_t)[1](d_act)[0]
     grad_table = dot(onehot.astype(F32), d_cond, 0, 1, HIGH)
     grad_bt_two = jnp.sum(d_cond, axis=1)
     d_cond_low = d_cond.astype(BF)
-    d_cond_t = exchange(
-        jnp.broadcast_to(d_cond_low[None], (n_all,) + d_cond_low.shape), ALL
-    ).reshape(D, n_all)
+    d_cond_t = to_all(d_cond_low, ALL).reshape(D, n_all)
     d_hidden = dot(temb_low[:, FREQ:], d_cond_t, 1, 0)
     d_pre_time = jax.vjp(jax.nn.silu, pre_t)[1](d_hidden)[0]
     grad_bt_one = lax.dynamic_slice_in_dim(
@@ -501,50 +680,39 @@
         axis=0,
     )
     n_small = small.shape[0]
-    small_sent = (
-        jnp.pad(small, ((0, 64 - n_small), (0, 0))).T.reshape(n_all, vec_cols, 64)
-    )
+    small_sent = jnp.pad(small, ((0, lanes - n_small), (0, 0))).T.reshape(n_all, vec_cols, lanes)
     small_own = jnp.sum(exchange(small_sent, ALL), axis=0).T
     vec_s = jnp.concatenate(
         [small_own[:1], grad_bt_one[None], grad_bt_two[None], small_own[1:17]], axis=0
     )
     io_s = small_own[17:n_small].reshape(2, PATCH, vec_cols)
 
-    grads_sent = jnp.concatenate(
-        [
-            attn_zg.reshape(n_plane // 2, RB, 4, 2, quarter)
-            .transpose(0, 3, 1, 2, 4)
-            .reshape(n_plane // 2, 2, RB, 4 * quarter),
-            jnp.stack(
-                [
-                    first_z.reshape(n_plane // 2, RB, wide),
-                    second_z.reshape(n_plane // 2, RB, wide),
-                ],
-                axis=1,
-            ),
-        ],
-        axis=3,
-    ).reshape(n_plane, RB, 4 * quarter + wide)
-    grads_own = jnp.sum(exchange(grads_sent, PLANE).astype(F32), axis=0)
-    attn_q = grads_own[:, : 4 * quarter].reshape(RB, 4, quarter).transpose(1, 0, 2)
-    mlp_q = grads_own[:, 4 * quarter :].reshape(RB, 4, half).transpose(1, 0, 2)
+    mod_c = in_order(core, grad_mod, swap(grad_mod, "c"), 0)
+    mod_s = in_order(yl, mod_c, swap(mod_c, "yl"), 0)
+    attn_q = jnp.sum(attn_back.astype(F32), axis=0)
+    mlp_q = jnp.stack(
+        [jnp.sum(first_back.astype(F32), axis=0), jnp.sum(second_back.astype(F32), axis=0)]
+    )
+    grads_square = jnp.sum(attn_q * attn_q) + jnp.sum(mlp_q * mlp_q)
+    attn_q = attn_q.reshape(RB, 4, quarter).transpose(1, 0, 2)
     attn_s = in_order(core, attn_q, swap(attn_q, "c"), 2)
-    mlp_s = in_order(yl, mlp_q, swap(mlp_q, "yl"), 0)
-    mod_s = lax.all_gather(
-        lax.all_gather(grad_mod, "c", axis=0, tiled=True), "yl", axis=0, tiled=True
+    mlp_s = (
+        in_order(yl, mlp_q, swap(mlp_q, "yl"), 2)
+        .reshape(2, RB, 4, half)
+        .transpose(0, 2, 1, 3)
+        .reshape(8, RB, half)
     )
 
     local_square = (
-        jnp.sum(grads_own * grads_own)
-        + jnp.sum(grad_mod * grad_mod)
-        + 0.25 * jnp.sum(grad_temb * grad_temb)
+        grads_square
+        + 0.25 * (jnp.sum(mod_s * mod_s) + jnp.sum(grad_temb * grad_temb))
         + jnp.sum(grad_table * grad_table)
         + jnp.sum(io_s * io_s)
         + jnp.sum(vec_s * vec_s)
     )
     sums = jnp.concatenate([local_square[None], loss_own[None], grad_hb])
     sums = jnp.pad(sums, (0, 128 - sums.shape[0]))
-    sums = jnp.sum(exchange(jnp.broadcast_to(sums[None], (n_all, 128)), ALL), axis=0)
+    sums = jnp.sum(to_all(sums[None], ALL), axis=0)[0]
     loss = sums[1] / count_all
     head_all = sums[2 : 2 + PATCH]
     grad_norm = jnp.sqrt(sums[0] + jnp.sum(head_all * head_all))

time: 654 us -> 639 us (0.977)
  waiting for transfers between devices: 230 us -> 128 us
  starting transfers between devices: 88.2 us -> 190 us
  blocking collectives: 52.3 us -> 0 us
  other arithmetic: 41.6 us -> 74.4 us
  matrix products: 119 us -> 90.7 us
  Pallas kernels: 5.44 us -> 22.9 us
  local copies, waits for them, and re-layouts: 75.7 us -> 89.9 us
    ppermute x0 -> x37, starting transfers between devices: none -> 63.1 us  [shift(): return lax.ppermute(v, axes, [(i, (i + by) % size) for i in range(size)])]
    all_gather x3 -> x1, waiting for transfers between devices: 62.8 us -> 0.02 us  [on_device(): second_mine = lax.all_gather(second_y, 'z', axis=0, tiled=True)]
    reduce_scatter x1, waiting for transfers between devices: 49.2 us -> 0.02 us  [on_device(): lax.psum_scatter(second_sum, 'z', scatter_dimension=0, tiled=True)]
    dot_general x12 -> x0, matrix products: 35.4 us -> none  [the longest x2 10.6 us: attend_back(): jnp.einsum('hqk,khd->qhd', d_raw, heads_of(k_low), preferred_element_type...]
    all_to_all x9 -> x11, starting transfers between devices: 80.5 us -> 111 us  [exchange(): return lax.all_to_all(v, axes, 0, 0)]
    all_to_all x1 -> x0, blocking collectives: 29 us -> none  [exchange(): return lax.all_to_all(v, axes, 0, 0, tiled=True)]
    ppermute x0 -> x37, waiting for transfers between devices: none -> 26.7 us  [shift(): return lax.ppermute(v, axes, [(i, (i + by) % size) for i in range(size)])]
    all_to_all x9 -> x11, waiting for transfers between devices: 104 us -> 77.1 us  [exchange(): return lax.all_to_all(v, axes, 0, 0)]
  transfers between devices with their start and end apart: 25 -> 64, of which waited for: 11 -> 19; matrix products, arithmetic and copies ran while one was open for 23% -> 34% of each run, Pallas kernels for 0% -> 3%
where the time goes in v1:
time: 639 us; the launch traced here: 628 us
  starting transfers between devices  190 us (30%)
  waiting for transfers between devices  128 us (20%)
  matrix products  90.7 us (14%)
  local copies, waits for them, and re-layouts  89.9 us (14%)
  other arithmetic  74.4 us (12%)
  between operations  31.1 us (5%)
  Pallas kernels  22.9 us (4%)
    all_to_all x11, starting transfers between devices, exchange(): return lax.all_to_all(v, axes, 0, 0)  111 us
    dot_general x46, matrix products, dot(): lax.dot_general(lhs, rhs, (((lhs_dim,), (rhs_dim,)), ((), ())), precision...  89.3 us
    all_to_all x11, waiting for transfers between devices, exchange(): return lax.all_to_all(v, axes, 0, 0)  77.1 us
    ppermute x37, starting transfers between devices, shift(): return lax.ppermute(v, axes, [(i, (i + by) % size) for i in range(size)])  63.1 us
    ppermute x37, waiting for transfers between devices, shift(): return lax.ppermute(v, axes, [(i, (i + by) % size) for i in range(size)])  26.7 us
    unnamed x254, local copies, waits for them, and re-layouts  25.3 us
    ppermute x14, waiting for transfers between devices, swap(): return lax.ppermute(v, axis, [(0, 1), (1, 0)])  24.3 us
    ppermute x14, starting transfers between devices, swap(): return lax.ppermute(v, axis, [(0, 1), (1, 0)])  16.1 us
  transfers between devices with their start and end apart: 64, of which 19 were waited for; matrix products, arithmetic and copies ran while one was open for 34% of the time, Pallas kernels for 3%

profile of v1, /device:TPU:1, one launch (start us, length us, event | category | flops | bytes accessed | tf_op | source)
XLA Modules:
  0.0 627.7 jit_solution(7331814264932558782)
XLA Ops:
  33.4 11.1 %all-to-all-start = ((bf16[256,4,128]{2,1,0:T(4,128)(2,1)}), bf16[256,4,128]{2,1,0:T(4,128)(2,1)S(1)}, u32[]{:S(2)}, u32[]{:S(2)}) async-start(bf16[256,4,128]{2,1,0:T(4,128)(2,1)} %maximum_maximum_fusion), calls=%async_computation | async-start | bytes 524288 | tf_op jit(solution)/shard_map/all_to_all | solution.py:60
  98.2 5.8 collective-permute-done.15
  116.5 8.0 %all-to-all-start.1 = ((f32[64,4,256]{2,1,0:T(4,128)}), f32[64,4,256]{2,1,0:T(4,128)S(1)}, u32[]{:S(2)}, u32[]{:S(2)}) async-start(f32[64,4,256]{2,1,0:T(4,128)} %copy.368), calls=%async_computation.1 | async-start | bytes 524288 | tf_op jit(solution)/shard_map/all_to_all | solution.py:60
  140.8 21.1 %all-to-all-start.2 = ((bf16[256,4,256]{2,1,0:T(4,128)(2,1)}), bf16[256,4,256]{2,1,0:T(4,128)(2,1)}, u32[]{:S(2)}, u32[]{:S(2)}) async-start(bf16[256,4,256]{2,1,0:T(4,128)(2,1)} %broadcast_in_dim.89), calls=%async_computation.2 | async-start | bytes 1048576 | tf_op jit(solution)/shard_map/all_to_all | solution.py:60
  176.6 7.8 %collective-permute-done.27 = bf16[4,1,64,1024]{3,2,0,1:T(8,128)(2,1)S(1)} collective-permute-done((bf16[4,1,64,1024]{3,2,0,1:T(8,128)(2,1)S(1)}, bf16[4,1,64,1024]{3,2,0,1:T(8,128)(2,1)S(1)}, u32[]{:S(2)}, u32[]{:S(2)}) %collective-permute-start.27) | collective-permute-done | bytes 524320 | tf_op jit(solution)/shard_map/ppermute | solution.py:77
  198.7 11.8 %all-to-all-start.3 = ((f32[256,1,32]{2,1,0:T(1,128)}), f32[256,1,32]{2,1,0:T(1,128)}, u32[]{:S(2)}, u32[]{:S(2)}) async-start(f32[256,1,32]{2,1,0:T(1,128)} %copy.384), calls=%async_computation.3 | async-start | bytes 262144 | tf_op jit(solution)/shard_map/all_to_all | solution.py:60
  216.6 6.1 all-to-all-done.3
  226.8 4.0 fusion.6.refs_0_.refs_1_.refs_2_
  234.5 6.4 %shard_map.440 = (bf16[256,512]{1,0:T(8,128)(2,1)}, bf16[256,512]{1,0:T(8,128)(2,1)}) custom-call(bf16[256,1536]{1,0:T(8,128)(2,1)} %fusion.6.refs_0_.refs_1_.refs_2_, bf16[256,1536]{1,0:T(8,128)(2,1)} %fusion.6.refs_0_.refs_1_.refs_2_, bf16[256,1536]{1,0:T(8,128)(2,1)} %fusion.6.refs_0_.refs_1_.refs_2_, ...), custom_call_target="tpu_custom_call" | custom-call | flops 536870912 | bytes 2097152 | tf_op jit(solution)/shard_map/pallas_call | solution.py:322
  249.7 4.2 convolution_add_fusion.2
  269.3 4.8 fusion.132
  277.7 4.3 fusion.115
  285.8 4.3 fusion.113
  290.1 3.9 fusion.51
  294.1 4.6 multiply_reduce_fusion.3
  314.4 6.5 %collective-permute-done.34 = bf16[4,1,64,1024]{3,2,1,0:T(8,128)(2,1)S(1)} collective-permute-done((bf16[4,1,64,1024]{3,2,1,0:T(8,128)(2,1)S(1)}, bf16[4,1,64,1024]{3,2,1,0:T(8,128)(2,1)S(1)}, u32[]{:S(2)}, u32[]{:S(2)}) %collective-permute-start.34) | collective-permute-done | bytes 524320 | tf_op jit(solution)/shard_map/ppermute | solution.py:77
  321.7 11.1 %shard_map.441 = (bf16[256,1536]{1,0:T(8,128)(2,1)}, bf16[256,1536]{1,0:T(8,128)(2,1)}) custom-call(bf16[256,1536]{1,0:T(8,128)(2,1)} %fusion.6.refs_0_.refs_1_.refs_2_, bf16[256,1536]{1,0:T(8,128)(2,1)} %fusion.6.refs_0_.refs_1_.refs_2_, bf16[256,1536]{1,0:T(8,128)(2,1)} %fusion.6.refs_0_.refs_1_.refs_2_, ...), custom_call_target="tpu_custom_call" | custom-call | flops 1342177280 | bytes 3670016 | tf_op jit(solution)/shard_map/pallas_call | solution.py:339
  355.1 4.6 multiply_reduce_fusion
  363.3 6.9 %all-to-all-start.7 = ((bf16[256,16,128]{2,1,0:T(8,128)(2,1)}), bf16[256,16,128]{2,1,0:T(8,128)(2,1)}, u32[]{:S(2)}, u32[]{:S(2)}) async-start(bf16[256,16,128]{2,1,0:T(8,128)(2,1)} %bitcast.75), calls=%async_computation.8 | async-start | bytes 2097152 | tf_op jit(solution)/shard_map/all_to_all | solution.py:60
  382.5 18.3 %all-to-all-done.7 = bf16[256,16,128]{2,1,0:T(8,128)(2,1)} async-done(((bf16[256,16,128]{2,1,0:T(8,128)(2,1)}), bf16[256,16,128]{2,1,0:T(8,128)(2,1)}, u32[]{:S(2)}, u32[]{:S(2)}) %all-to-all-start.7) | async-done | bytes 1048608 | tf_op jit(solution)/shard_map/all_to_all | solution.py:60
  400.8 6.9 %all-to-all-start.9 = ((f32[256,4,128]{2,1,0:T(4,128)}), f32[256,4,128]{2,1,0:T(4,128)}, u32[]{:S(2)}, u32[]{:S(2)}) async-start(f32[256,4,128]{2,1,0:T(4,128)} %bitcast.326), calls=%async_computation.10 | async-start | bytes 1048576 | tf_op jit(solution)/shard_map/all_to_all | solution.py:60
  422.7 17.5 %collective-permute-done.46 = f32[16,256]{1,0:T(8,128)S(1)} collective-permute-done((f32[16,256]{1,0:T(8,128)S(1)}, f32[16,256]{1,0:T(8,128)S(1)}, u32[]{:S(2)}, u32[]{:S(2)}) %collective-permute-start.46) | collective-permute-done | bytes 16416 | tf_op jit(solution)/shard_map/ppermute | solution.py:72
  441.3 12.4 %all-to-all-start.8 = ((bf16[256,4,256]{2,1,0:T(4,128)(2,1)}), bf16[256,4,256]{2,1,0:T(4,128)(2,1)S(1)}, u32[]{:S(2)}, u32[]{:S(2)}) async-start(bf16[256,4,256]{2,1,0:T(4,128)(2,1)} %broadcast_in_dim.197), calls=%async_computation.9 | async-start | bytes 1048576 | tf_op jit(solution)/shard_map/all_to_all | solution.py:60
  461.1 12.8 %all-to-all-done.8 = bf16[256,4,256]{2,1,0:T(4,128)(2,1)S(1)} async-done(((bf16[256,4,256]{2,1,0:T(4,128)(2,1)}), bf16[256,4,256]{2,1,0:T(4,128)(2,1)S(1)}, u32[]{:S(2)}, u32[]{:S(2)}) %all-to-all-start.8) | async-done | bytes 524320 | tf_op jit(solution)/shard_map/all_to_all | solution.py:60
  483.6 9.8 %all-to-all-done.6 = bf16[16,16,1024]{2,1,0:T(8,128)(2,1)S(1)} async-done(((bf16[16,16,1024]{2,1,0:T(8,128)(2,1)}), bf16[16,16,1024]{2,1,0:T(8,128)(2,1)S(1)}, u32[]{:S(2)}, u32[]{:S(2)}) %all-to-all-start.6) | async-done | bytes 524320 | tf_op jit(solution)/shard_map/all_to_all | solution.py:60
  494.1 9.8 %all-to-all-start.5 = ((bf16[32,16,1024]{2,1,0:T(8,128)(2,1)}), bf16[32,16,1024]{2,1,0:T(8,128)(2,1)S(1)}, u32[]{:S(2)}, u32[]{:S(2)}) async-start(bf16[32,16,1024]{2,1,0:T(8,128)(2,1)} %bitcast.58), calls=%async_computation.5 | async-start | bytes 2097152 | tf_op jit(solution)/shard_map/all_to_all | solution.py:60
  512.5 17.1 %all-to-all-done.5 = bf16[32,16,1024]{2,1,0:T(8,128)(2,1)S(1)} async-done(((bf16[32,16,1024]{2,1,0:T(8,128)(2,1)}), bf16[32,16,1024]{2,1,0:T(8,128)(2,1)S(1)}, u32[]{:S(2)}, u32[]{:S(2)}) %all-to-all-start.5) | async-done | bytes 1048608 | tf_op jit(solution)/shard_map/all_to_all | solution.py:60
  529.6 5.4 all-to-all-start.4
  542.1 6.8 %collective-permute-done.44 = f32[4,16,1024]{2,1,0:T(8,128)S(1)} collective-permute-done((f32[4,16,1024]{2,1,0:T(8,128)S(1)}, f32[4,16,1024]{2,1,0:T(8,128)S(1)}, u32[]{:S(2)}, u32[]{:S(2)}) %collective-permute-start.44) | collective-permute-done | bytes 262176 | tf_op jit(solution)/shard_map/ppermute | solution.py:72
  565.0 14.1 %all-to-all-start.10 = ((f32[256,1,128]{2,1,0:T(1,128)}), f32[256,1,128]{2,1,0:T(1,128)S(1)}, u32[]{:S(2)}, u32[]{:S(2)}) async-start(f32[256,1,128]{2,1,0:T(1,128)} %broadcast_in_dim.207), calls=%async_computation.11 | async-start | bytes 262144 | tf_op jit(solution)/shard_map/all_to_all | solution.py:60
  581.6 10.2 %all-to-all-done.10 = f32[256,1,128]{2,1,0:T(1,128)S(1)} async-done(((f32[256,1,128]{2,1,0:T(1,128)}), f32[256,1,128]{2,1,0:T(1,128)S(1)}, u32[]{:S(2)}, u32[]{:S(2)}) %all-to-all-start.10) | async-done | bytes 131104 | tf_op jit(solution)/shard_map/all_to_all | solution.py:60
  605.0 5.4 shard_map.442
  (664 shorter events, 312.8 us)
Async XLA Ops:
  8.3 46.7 %collective-permute-start.2 = (bf16[1,16,1024]{2,1,0:T(8,128)(2,1)S(1)}, bf16[1,16,1024]{2,1,0:T(8,128)(2,1)S(1)}, u32[]{:S(2)}, u32[]{:S(2)}) collective-permute-start(bf16[1,16,1024]{2,1,0:T(8,128)(2,1)S(1)} %slice.315), channel_id=1, source_target_pairs={{0,4},{4,8},{8,12},{12,0},{1,5},{5,9},{9,13},{13,1},{2,6},{6,10},{... | collective-permute-start | bytes 98312 | tf_op jit(solution)/shard_map/ppermute | solution.py:77
  10.4 41.1 %collective-permute-start.1 = (bf16[1,16,1024]{2,1,0:T(8,128)(2,1)S(1)}, bf16[1,16,1024]{2,1,0:T(8,128)(2,1)S(1)}, u32[]{:S(2)}, u32[]{:S(2)}) collective-permute-start(bf16[1,16,1024]{2,1,0:T(8,128)(2,1)S(1)} %slice.315), channel_id=1, source_target_pairs={{0,8},{4,12},{8,0},{12,4},{1,9},{5,13},{9,1},{13,5},{2,10},{6,14},... | collective-permute-start | bytes 98312 | tf_op jit(solution)/shard_map/ppermute | solution.py:77
  12.9 34.7 %collective-permute-start = (bf16[1,16,1024]{2,1,0:T(8,128)(2,1)S(1)}, bf16[1,16,1024]{2,1,0:T(8,128)(2,1)S(1)}, u32[]{:S(2)}, u32[]{:S(2)}) collective-permute-start(bf16[1,16,1024]{2,1,0:T(8,128)(2,1)S(1)} %slice.315), channel_id=1, source_target_pairs={{0,12},{4,0},{8,4},{12,8},{1,13},{5,1},{9,5},{13,9},{2,14},{6,2},{... | collective-permute-start | bytes 98312 | tf_op jit(solution)/shard_map/ppermute | solution.py:77
  14.9 62.6 %collective-permute-start.12 = (bf16[1,16,2048]{2,1,0:T(8,128)(2,1)S(1)}, bf16[1,16,2048]{2,1,0:T(8,128)(2,1)S(1)}, u32[]{:S(2)}, u32[]{:S(2)}) collective-permute-start(bf16[1,16,2048]{2,1,0:T(8,128)(2,1)S(1)} %maximum_bitcast_fusion.7), channel_id=1, source_target_pairs={{0,32},{32,64},{64,96},{96,128},{128,160},{160,192},{192,224},{224... | collective-permute-start | bytes 196616 | tf_op jit(solution)/shard_map/ppermute | solution.py:77
  16.6 60.3 %collective-permute-start.11 = (bf16[1,16,2048]{2,1,0:T(8,128)(2,1)S(1)}, bf16[1,16,2048]{2,1,0:T(8,128)(2,1)S(1)}, u32[]{:S(2)}, u32[]{:S(2)}) collective-permute-start(bf16[1,16,2048]{2,1,0:T(8,128)(2,1)S(1)} %maximum_bitcast_fusion.7), channel_id=1, source_target_pairs={{0,64},{32,96},{64,128},{96,160},{128,192},{160,224},{192,0},{224,... | collective-permute-start | bytes 196616 | tf_op jit(solution)/shard_map/ppermute | solution.py:77
  33.4 73.7 %all-to-all-start = ((bf16[256,4,128]{2,1,0:T(4,128)(2,1)}), bf16[256,4,128]{2,1,0:T(4,128)(2,1)S(1)}, u32[]{:S(2)}, u32[]{:S(2)}) async-start(bf16[256,4,128]{2,1,0:T(4,128)(2,1)} %maximum_maximum_fusion), calls=%async_computation | async-start | bytes 524288 | tf_op jit(solution)/shard_map/all_to_all | solution.py:60
  44.5 166.1 %all-gather.2.cloned.1.call-start = ((), (), s32[]{:S(2)}) async-start(), calls=%async_computation.12 | async-start | bytes 4718592 | tf_op jit(solution)/shard_map/all_gather | solution.py:404
  47.6 27.6 %collective-permute-start.10 = (bf16[1,16,2048]{2,1,0:T(8,128)(2,1)S(1)}, bf16[1,16,2048]{2,1,0:T(8,128)(2,1)S(1)}, u32[]{:S(2)}, u32[]{:S(2)}) collective-permute-start(bf16[1,16,2048]{2,1,0:T(8,128)(2,1)S(1)} %maximum_bitcast_fusion.7), channel_id=1, source_target_pairs={{0,96},{32,128},{64,160},{96,192},{128,224},{160,0},{192,32},{224,... | collective-permute-start | bytes 196616 | tf_op jit(solution)/shard_map/ppermute | solution.py:77
  107.1 54.8 %collective-permute-start.22 = (bf16[16,1,16,2048]{3,2,0,1:T(8,128)(2,1)}, bf16[16,1,16,2048]{3,2,0,1:T(8,128)(2,1)}, u32[]{:S(2)}, u32[]{:S(2)}) collective-permute-start(bf16[16,1,16,2048]{3,2,0,1:T(8,128)(2,1)} %bitcast.29), channel_id=1, source_target_pairs={{0,4},{4,8},{8,12},{12,0},{1,5},{5,9},{9,13},{13,1},{2,6},{6,10},{... | collective-permute-start | bytes 3145736 | tf_op jit(solution)/shard_map/ppermute | solution.py:77
  107.1 57.4 %collective-permute-start.21 = (bf16[16,1,16,2048]{3,2,0,1:T(8,128)(2,1)}, bf16[16,1,16,2048]{3,2,0,1:T(8,128)(2,1)}, u32[]{:S(2)}, u32[]{:S(2)}) collective-permute-start(bf16[16,1,16,2048]{3,2,0,1:T(8,128)(2,1)} %bitcast.29), channel_id=1, source_target_pairs={{0,12},{4,0},{8,4},{12,8},{1,13},{5,1},{9,5},{13,9},{2,14},{6,2},{... | collective-permute-start | bytes 3145736 | tf_op jit(solution)/shard_map/ppermute | solution.py:77
  109.8 57.2 %collective-permute-start.26 = (bf16[8,1,64,1024]{3,2,0,1:T(8,128)(2,1)}, bf16[8,1,64,1024]{3,2,0,1:T(8,128)(2,1)}, u32[]{:S(2)}, u32[]{:S(2)}) collective-permute-start(bf16[8,1,64,1024]{3,2,0,1:T(8,128)(2,1)} %bitcast.35), channel_id=1, source_target_pairs={{0,2},{2,16},{16,18},{18,0},{1,3},{3,17},{17,19},{19,1},{4,6},{6,2... | collective-permute-start | bytes 3145736 | tf_op jit(solution)/shard_map/ppermute | solution.py:77
  109.8 59.7 %collective-permute-start.25 = (bf16[8,1,64,1024]{3,2,0,1:T(8,128)(2,1)}, bf16[8,1,64,1024]{3,2,0,1:T(8,128)(2,1)}, u32[]{:S(2)}, u32[]{:S(2)}) collective-permute-start(bf16[8,1,64,1024]{3,2,0,1:T(8,128)(2,1)} %bitcast.35), channel_id=1, source_target_pairs={{0,18},{2,0},{16,2},{18,16},{1,19},{3,1},{17,3},{19,17},{4,22},{6,... | collective-permute-start | bytes 3145736 | tf_op jit(solution)/shard_map/ppermute | solution.py:77
  140.8 51.1 %all-to-all-start.2 = ((bf16[256,4,256]{2,1,0:T(4,128)(2,1)}), bf16[256,4,256]{2,1,0:T(4,128)(2,1)}, u32[]{:S(2)}, u32[]{:S(2)}) async-start(bf16[256,4,256]{2,1,0:T(4,128)(2,1)} %broadcast_in_dim.89), calls=%async_computation.2 | async-start | bytes 1048576 | tf_op jit(solution)/shard_map/all_to_all | solution.py:60
  191.8 38.9 %collective-permute-start.29 = (bf16[1024,2048]{1,0:T(8,128)(2,1)}, bf16[1024,2048]{1,0:T(8,128)(2,1)}, u32[]{:S(2)}, u32[]{:S(2)}) collective-permute-start(bf16[1024,2048]{1,0:T(8,128)(2,1)} %bitcast.40), channel_id=1, source_target_pairs={{0,1},{1,0},{2,3},{3,2},{4,5},{5,4},{6,7},{7,6},{8,9},{9,8},{10,11... | collective-permute-start | bytes 12582920 | tf_op jit(solution)/shard_map/ppermute | solution.py:72
  193.6 56.0 %collective-permute-start.30 = (bf16[1024,2048]{1,0:T(8,128)(2,1)}, bf16[1024,2048]{1,0:T(8,128)(2,1)}, u32[]{:S(2)}, u32[]{:S(2)}) collective-permute-start(bf16[1024,2048]{1,0:T(8,128)(2,1)} %bitcast.45), channel_id=1, source_target_pairs={{0,1},{1,0},{2,3},{3,2},{4,5},{5,4},{6,7},{7,6},{8,9},{9,8},{10,11... | collective-permute-start | bytes 12582920 | tf_op jit(solution)/shard_map/ppermute | solution.py:72
  210.5 243.2 %reduce-scatter.2.cloned.1.call-start = ((), (), s32[]{:S(2)}) async-start(), calls=%async_computation.13 | async-start | bytes 4718592 | tf_op jit(solution)/shard_map/reduce_scatter | solution.py:556
  210.6 44.9 %collective-permute-start.31 = (bf16[1024,2048]{1,0:T(8,128)(2,1)}, bf16[1024,2048]{1,0:T(8,128)(2,1)}, u32[]{:S(2)}, u32[]{:S(2)}) collective-permute-start(bf16[1024,2048]{1,0:T(8,128)(2,1)} %all-gather.2.cloned.1.call-done), channel_id=1, source_target_pairs={{0,1},{1,0},{2,3},{3,2},{4,5},{5,4},{6,7},{7,6},{8,9},{9,8},{10,11... | collective-permute-start | bytes 12582920 | tf_op jit(solution)/shard_map/ppermute | solution.py:72
  337.6 77.1 %collective-permute-start.36 = (bf16[1024,2048]{1,0:T(8,128)(2,1)}, bf16[1024,2048]{1,0:T(8,128)(2,1)}, u32[]{:S(2)}, u32[]{:S(2)}) collective-permute-start(bf16[1024,2048]{1,0:T(8,128)(2,1)} %pad_maximum_fusion), channel_id=1, source_target_pairs={{0,1},{1,0},{2,3},{3,2},{4,5},{5,4},{6,7},{7,6},{8,9},{9,8},{10,11... | collective-permute-start | bytes 12582920 | tf_op jit(solution)/shard_map/ppermute | solution.py:72
  363.3 37.5 %all-to-all-start.7 = ((bf16[256,16,128]{2,1,0:T(8,128)(2,1)}), bf16[256,16,128]{2,1,0:T(8,128)(2,1)}, u32[]{:S(2)}, u32[]{:S(2)}) async-start(bf16[256,16,128]{2,1,0:T(8,128)(2,1)} %bitcast.75), calls=%async_computation.8 | async-start | bytes 2097152 | tf_op jit(solution)/shard_map/all_to_all | solution.py:60
  378.8 101.3 %collective-permute-start.42 = (bf16[8,1,64,1024]{3,2,1,0:T(8,128)(2,1)}, bf16[8,1,64,1024]{3,2,1,0:T(8,128)(2,1)}, u32[]{:S(2)}, u32[]{:S(2)}) collective-permute-start(bf16[8,1,64,1024]{3,2,1,0:T(8,128)(2,1)} %pad_maximum_fusion.6), channel_id=1, source_target_pairs={{0,18},{2,0},{16,2},{18,16},{1,19},{3,1},{17,3},{19,17},{4,22},{6,... | collective-permute-start | bytes 3145736 | tf_op jit(solution)/shard_map/ppermute | solution.py:77
  400.8 39.6 %all-to-all-start.9 = ((f32[256,4,128]{2,1,0:T(4,128)}), f32[256,4,128]{2,1,0:T(4,128)}, u32[]{:S(2)}, u32[]{:S(2)}) async-start(f32[256,4,128]{2,1,0:T(4,128)} %bitcast.326), calls=%async_computation.10 | async-start | bytes 1048576 | tf_op jit(solution)/shard_map/all_to_all | solution.py:60
  413.9 66.2 %collective-permute-start.41 = (bf16[8,1,64,1024]{3,2,1,0:T(8,128)(2,1)}, bf16[8,1,64,1024]{3,2,1,0:T(8,128)(2,1)}, u32[]{:S(2)}, u32[]{:S(2)}) collective-permute-start(bf16[8,1,64,1024]{3,2,1,0:T(8,128)(2,1)} %pad_maximum_fusion.5), channel_id=1, source_target_pairs={{0,2},{2,16},{16,18},{18,0},{1,3},{3,17},{17,19},{19,1},{4,6},{6,2... | collective-permute-start | bytes 3145736 | tf_op jit(solution)/shard_map/ppermute | solution.py:77
  413.9 26.3 %collective-permute-start.46 = (f32[16,256]{1,0:T(8,128)S(1)}, f32[16,256]{1,0:T(8,128)S(1)}, u32[]{:S(2)}, u32[]{:S(2)}) collective-permute-start(f32[16,256]{1,0:T(8,128)S(1)} %add.735), channel_id=1, source_target_pairs={{0,2},{2,0},{1,3},{3,1},{4,6},{6,4},{5,7},{7,5},{8,10},{10,8},{9,1... | collective-permute-start | bytes 49160 | tf_op jit(solution)/shard_map/ppermute | solution.py:72
  419.8 35.8 %collective-permute-start.37 = (bf16[8,1,16,2048]{3,2,0,1:T(8,128)(2,1)}, bf16[8,1,16,2048]{3,2,0,1:T(8,128)(2,1)S(1)}, u32[]{:S(2)}, u32[]{:S(2)}) collective-permute-start(bf16[8,1,16,2048]{3,2,0,1:T(8,128)(2,1)} %get-tuple-element.338), channel_id=1, source_target_pairs={{0,4},{4,8},{8,12},{12,0},{1,5},{5,9},{9,13},{13,1},{2,6},{6,10},{... | collective-permute-start | bytes 1572872 | tf_op jit(solution)/shard_map/ppermute | solution.py:77
  421.2 34.5 %collective-permute-start.39 = (bf16[8,1,16,2048]{3,2,0,1:T(8,128)(2,1)S(1)}, bf16[8,1,16,2048]{3,2,0,1:T(8,128)(2,1)}, u32[]{:S(2)}, u32[]{:S(2)}) collective-permute-start(bf16[8,1,16,2048]{3,2,0,1:T(8,128)(2,1)S(1)} %get-tuple-element.340), channel_id=1, source_target_pairs={{0,12},{4,0},{8,4},{12,8},{1,13},{5,1},{9,5},{13,9},{2,14},{6,2},{... | collective-permute-start | bytes 1572872 | tf_op jit(solution)/shard_map/ppermute | solution.py:77
  441.3 32.6 %all-to-all-start.8 = ((bf16[256,4,256]{2,1,0:T(4,128)(2,1)}), bf16[256,4,256]{2,1,0:T(4,128)(2,1)S(1)}, u32[]{:S(2)}, u32[]{:S(2)}) async-start(bf16[256,4,256]{2,1,0:T(4,128)(2,1)} %broadcast_in_dim.197), calls=%async_computation.9 | async-start | bytes 1048576 | tf_op jit(solution)/shard_map/all_to_all | solution.py:60
  458.5 50.0 %collective-permute-start.40 = (bf16[16,1,16,2048]{3,2,0,1:T(8,128)(2,1)}, bf16[16,1,16,2048]{3,2,0,1:T(8,128)(2,1)}, u32[]{:S(2)}, u32[]{:S(2)}) collective-permute-start(bf16[16,1,16,2048]{3,2,0,1:T(8,128)(2,1)} %pad_maximum_fusion.3), channel_id=1, source_target_pairs={{0,12},{4,0},{8,4},{12,8},{1,13},{5,1},{9,5},{13,9},{2,14},{6,2},{... | collective-permute-start | bytes 3145736 | tf_op jit(solution)/shard_map/ppermute | solution.py:77
  478.7 30.1 %collective-permute-start.38 = (bf16[16,1,16,2048]{3,2,0,1:T(8,128)(2,1)}, bf16[16,1,16,2048]{3,2,0,1:T(8,128)(2,1)}, u32[]{:S(2)}, u32[]{:S(2)}) collective-permute-start(bf16[16,1,16,2048]{3,2,0,1:T(8,128)(2,1)} %pad_maximum_fusion.2), channel_id=1, source_target_pairs={{0,4},{4,8},{8,12},{12,0},{1,5},{5,9},{9,13},{13,1},{2,6},{6,10},{... | collective-permute-start | bytes 3145736 | tf_op jit(solution)/shard_map/ppermute | solution.py:77
  494.1 35.5 %all-to-all-start.5 = ((bf16[32,16,1024]{2,1,0:T(8,128)(2,1)}), bf16[32,16,1024]{2,1,0:T(8,128)(2,1)S(1)}, u32[]{:S(2)}, u32[]{:S(2)}) async-start(bf16[32,16,1024]{2,1,0:T(8,128)(2,1)} %bitcast.58), calls=%async_computation.5 | async-start | bytes 2097152 | tf_op jit(solution)/shard_map/all_to_all | solution.py:60
  507.0 30.0 %collective-permute-start.43 = (f32[2,16,1024]{2,1,0:T(8,128)S(1)}, f32[2,16,1024]{2,1,0:T(8,128)S(1)}, u32[]{:S(2)}, u32[]{:S(2)}) collective-permute-start(f32[2,16,1024]{2,1,0:T(8,128)S(1)} %convolution_bitcast_fusion), channel_id=1, source_target_pairs={{0,1},{1,0},{2,3},{3,2},{4,5},{5,4},{6,7},{7,6},{8,9},{9,8},{10,11... | collective-permute-start | bytes 393224 | tf_op jit(solution)/shard_map/ppermute | solution.py:72
  529.6 30.0 %all-to-all-start.4 = ((bf16[32,16,1024]{2,1,0:T(8,128)(2,1)}), bf16[32,16,1024]{2,1,0:T(8,128)(2,1)S(1)}, u32[]{:S(2)}, u32[]{:S(2)}) async-start(bf16[32,16,1024]{2,1,0:T(8,128)(2,1)} %bitcast.57), calls=%async_computation.4 | async-start | bytes 2097152 | tf_op jit(solution)/shard_map/all_to_all | solution.py:60
  565.0 26.8 %all-to-all-start.10 = ((f32[256,1,128]{2,1,0:T(1,128)}), f32[256,1,128]{2,1,0:T(1,128)S(1)}, u32[]{:S(2)}, u32[]{:S(2)}) async-start(f32[256,1,128]{2,1,0:T(1,128)} %broadcast_in_dim.207), calls=%async_computation.11 | async-start | bytes 262144 | tf_op jit(solution)/shard_map/all_to_all | solution.py:60
  (142 other events, 1708.5 us)
Sparse Core Ops, SparseCore 0:
  92.7 65.1 all-gather.1
  285.9 49.0 reduce-scatter.1

commit v2 on v1

--- a/solution.py
+++ b/solution.py
@@ -72,63 +72,12 @@
     return lax.ppermute(v, axis, [(0, 1), (1, 0)])
 
 
-def shift(v, axes, by):
-    size = lax.axis_size(axes)
-    return lax.ppermute(v, axes, [(i, (i + by) % size) for i in range(size)])
-
-
-def gather_first(v, axes):
-    if lax.axis_size(axes) == 2:
-        return (shift(v, axes, 1),)
-    return shift(v, axes, 1), shift(v, axes, -1)
-
-
-def gather_rest(v, axes, got):
-    if lax.axis_size(axes) == 2:
-        return (v,) + got
-    before, next_ = got
-    cut = v.shape[0] // 2
-    across = jnp.concatenate([shift(before[:cut], axes, 1), shift(next_[cut:], axes, -1)], axis=0)
-    return v, next_, across, before
-
-
 def all_after(values, *others):
     return lax.optimization_barrier(tuple(values) + others)[: len(values)]
 
 
-def reduce_first(piece, axes):
-    if lax.axis_size(axes) == 2:
-        return ()
-    across = piece(2)
-    cut = across.shape[0] // 2
-    return shift(across[:cut], axes, 1), shift(across[cut:], axes, -1)
-
-
-def reduce_rest(piece, axes, got):
-    if lax.axis_size(axes) == 2:
-        return piece(0).astype(F32) + shift(piece(1), axes, 1).astype(F32)
-    from_before, from_after = got
-    cut = from_before.shape[0]
-    up, down = piece(1), piece(3)
-    up = jnp.concatenate([added(up[:cut], from_before), up[cut:]], axis=0)
-    down = jnp.concatenate([down[:cut], added(down[cut:], from_after)], axis=0)
-    from_before = shift(up, axes, 1).astype(F32)
-    from_after = shift(down, axes, -1).astype(F32)
-    return piece(0).astype(F32) + from_before + from_after
-
-
 def added(one, two):
     return (one.astype(F32) + two.astype(F32)).astype(BF)
-
-
-def placed(blocks, index, size, axis):
-    shape = list(blocks[0].shape)
-    shape[axis] *= size
-    out = jnp.zeros(shape, blocks[0].dtype)
-    for r, block in enumerate(blocks):
-        where = lax.rem(index + r, size) * blocks[0].shape[axis]
-        out = lax.dynamic_update_slice_in_dim(out, block, where, axis)
-    return out
 
 
 def in_order(index, mine, other, axis):
@@ -137,15 +86,6 @@
         jnp.concatenate([mine, other], axis=axis),
         jnp.concatenate([other, mine], axis=axis),
     )
-
-
-def place_y(blocks, y_at):
-    first, _, rows, cols = blocks[0].shape
-    out = jnp.zeros((first, 2, rows, 2 * cols), blocks[0].dtype)
-    for r, block in enumerate(blocks):
-        where = lax.rem(y_at + r, 4)
-        out = lax.dynamic_update_slice(out, block, (0, where // 2, 0, where % 2 * cols))
-    return out
 
 
 def join_y(low, high):
@@ -163,17 +103,6 @@
             v[..., (6 + side) * width : (7 + side) * width],
         ],
         axis=-1,
-    )
-
-
-def gather_direct(v, axes):
-    return [v] + [shift(v, axes, -by) for by in range(1, lax.axis_size(axes))]
-
-
-def in_ring_order(blocks, index):
-    size = len(blocks)
-    return lax.dynamic_slice_in_dim(
-        jnp.concatenate(blocks + blocks, axis=0), lax.rem(size - index, size), size, axis=0
     )
 
 
@@ -385,10 +314,7 @@
     quarter = D // 4
     wide = 4 * half
 
-    n_z, n_x = lax.axis_size("z"), lax.axis_size("x")
-    x_at = lax.axis_index("x")
-    yh = lax.axis_index("yh")
-    y_at = 2 * yh + yl
+    n_x = lax.axis_size("x")
     attn_low = lax.dynamic_slice_in_dim(attn_w, core * quarter, quarter, axis=2).astype(BF)
     attn_own = attn_low.transpose(1, 0, 2).reshape(RB, 4 * quarter)
     mlp_low = (
@@ -397,13 +323,20 @@
         .transpose(0, 2, 1, 3)
         .reshape(2, RB, D)
     )
-    z_at = lax.axis_index("z")
-    second_x = in_ring_order(gather_direct(mlp_low[1][None], "x"), x_at)
-    second_parts = gather_direct(second_x.reshape(1, 1, n_x * RB, D), ("yh", "yl"))
-    second_y = place_y(second_parts, y_at).reshape(2 * n_x * RB, wide)
-    second_mine = lax.all_gather(second_y, "z", axis=0, tiled=True)
-    both_z = in_ring_order(
-        gather_direct(jnp.concatenate([attn_own, mlp_low[0]], axis=1)[None], "z"), z_at
+    plane_rows = to_all(jnp.concatenate([attn_own, mlp_low[0], mlp_low[1]], axis=1), PLANE)
+    plane_rows = plane_rows.reshape(2 * n_x, 2, RB, 3 * D)
+    low, high = plane_rows[:, 0], plane_rows[:, 1]
+    attn_mine = lax.all_gather(
+        join_y(low[..., :D], high[..., :D]).reshape(-1, wide), "z", axis=0, tiled=True
+    )
+    mlp_mine = lax.all_gather(
+        jnp.concatenate(
+            [low[..., D : 2 * D], high[..., D : 2 * D], low[..., 2 * D :], high[..., 2 * D :]],
+            axis=-1,
+        ).reshape(-1, 2 * wide),
+        "z",
+        axis=0,
+        tiled=True,
     )
 
     label_own = lax.dynamic_index_in_dim(labels, sub, keepdims=False)
@@ -439,20 +372,6 @@
         axis=2,
     )
     got = exchange(sent, ALL)
-    attn_own, first_own = both_z[..., :D], both_z[:, None, :, D:]
-    attn_got = gather_first(attn_own, ("yh", "yl"))
-    first_got = gather_first(first_own, "x")
-    low_y = yl == 0
-    own, next_, across, before = gather_rest(attn_own, ("yh", "yl"), attn_got)
-    pair_own = join_y(jnp.where(low_y, own, before), jnp.where(low_y, next_, own))
-    pair_far = join_y(jnp.where(low_y, across, next_), jnp.where(low_y, before, across))
-    attn_y = in_order(yh, pair_own[:, None], pair_far[:, None], 1).reshape(2 * n_z, 1, RB, wide)
-    first_x = placed(gather_rest(first_own, "x", first_got), x_at, n_x, 1).reshape(
-        n_z, 1, n_x * RB, D
-    )
-    attn_y, first_x = all_after((attn_y, first_x), got)
-    attn_got = gather_first(attn_y, "x")
-    first_got = gather_first(first_x, ("yh", "yl"))
     marks = got[:, 0, lanes_int : lanes_int + 4].astype(F32)
     labels_all = (marks[:, 0] * 32.0 + marks[:, 1]).astype(jnp.int32)
     times_all = marks[:, 2] * 32.0 + marks[:, 3]
@@ -477,31 +396,23 @@
     ).reshape(RB, n_shard * vec_cols)
     cond_parts = dot(temb_cols, hid_t, 0, 0)
     cond_parts = exchange(
-        after(cond_parts.reshape(n_shard, vec_cols, n_all), second_x), SHARD
+        cond_parts.reshape(n_shard, vec_cols, n_all), SHARD
     )
     onehot = (labels_all[:, None] == jnp.arange(NCLS)[None, :]).astype(BF)
     label_rows = dot(label_table.astype(BF), onehot, 0, 1)
     cond_t = jnp.sum(cond_parts, axis=0) + label_rows + rounded(vec_w[2])[:, None]
     act_own = jax.nn.silu(cond_t).astype(BF)
-    act_t = to_all(after(act_own, second_y), ALL)
-    attn_mine = placed(gather_rest(attn_y, "x", attn_got), x_at, n_x, 1).reshape(D, wide)
-    first_mine = place_y(gather_rest(first_x, ("yh", "yl"), first_got), y_at).reshape(D, wide)
+    act_t = to_all(act_own, ALL)
     patch_vals = lax.dynamic_index_in_dim(noisy_patches, sub, keepdims=False).reshape(SEQ, PATCH)
     x_in = dot(patch_vals, io_low[:PATCH], 1, 0) + vec_f[0] + grid_table()
     norm_one, inv_one = layer_norm(x_in)
-    act_t, attn_mine, first_mine, norm_one = lax.optimization_barrier(
-        (act_t, attn_mine, first_mine, norm_one)
-    )
+    act_t, attn_mine, norm_one = lax.optimization_barrier((act_t, attn_mine, norm_one))
+    attn_halves = (attn_mine, swap(attn_mine, "c"))
     act_t = act_t.reshape(D, n_all)
     mods_sent = dot(act_t, mod_col, 0, 0) + own_mod_bias.T.reshape(1, 2 * RB)
     mods = (
         exchange(mods_sent[:, None], ALL).reshape(n_shard, 8, RB).transpose(1, 0, 2).reshape(8, 1, D)
     )
-    second_mine = after(second_mine, mods)
-    attn_halves = (attn_mine, swap(attn_mine, "c"))
-    first_halves = (first_mine, swap(first_mine, "c"))
-    second_halves = (second_mine, swap(second_mine, "c"))
-
     target = lax.dynamic_index_in_dim(true_noise, sub, keepdims=False).reshape(SEQ, PATCH)
     head_low = rounded(head_b)
     h_one = (norm_one * (1.0 + mods[1]) + mods[0]).astype(BF)
@@ -518,6 +429,10 @@
         )
         qkv.append((dot(h_one, weight[:, : 3 * half], 1, 0) + bias.reshape(3 * half)).astype(BF))
     attended = attend(qkv)
+    mlp_mine = after(mlp_mine, attended[0])
+    mlp_halves = (mlp_mine, swap(mlp_mine, "c"))
+    first_halves = [m[:, :wide] for m in mlp_halves]
+    second_halves = [m[:, wide:] for m in mlp_halves]
     attn_out = vec_f[13]
     for weight, att in zip(attn_halves, attended):
         attn_out = attn_out + dot(att, weight[:, 3 * half :], 1, 1)
@@ -552,14 +467,12 @@
     d_mlp = mods[5] * d_two
     d_mlp_low = d_mlp.astype(BF)
     grad_bfc = jnp.sum(d_mlp, axis=0)
-    second_sum = chip_sum([dot(d_mlp_low, act, 0, 0).astype(BF) for act in act_mlp])
-    second_z = lax.psum_scatter(second_sum, "z", scatter_dimension=0, tiled=True).reshape(
-        2 * n_x, RB, wide
-    )
+    d_acts = [dot(d_mlp_low, second, 1, 0) for second in second_halves]
+    second_sum = chip_sum([dot(d_mlp_low, act, 0, 0).astype(BF) for act in act_mlp], *d_acts)
+    second_z = lax.psum_scatter(second_sum, "z", scatter_dimension=0, tiled=True)
     d_pre_low = []
     hid_bias = []
     d_h_two = 0.0
-    d_acts = [dot(d_mlp_low, second, 1, 0) for second in second_halves]
     d_acts = lax.optimization_barrier(tuple(d_acts) + (second_sum,))[:2]
     for pre, first, d_act in zip(pre_mlp, first_halves, d_acts):
         d_pre = jax.vjp(gelu_tanh, pre)[1](d_act)[0]
@@ -567,15 +480,7 @@
         d_pre_low.append(d_pre.astype(BF))
         d_h_two = d_h_two + dot(d_pre_low[-1], first, 1, 1)
     first_sum = chip_sum([dot(h_two, d, 0, 0).astype(BF) for d in d_pre_low])
-    first_parts = first_sum.reshape(n_z, 2, n_x * RB, wide)
-
-    def first_piece(r):
-        where = lax.rem(y_at + r, 4)
-        return lax.dynamic_slice(
-            first_parts, (0, where // 2, 0, where % 2 * D), (n_z, 1, n_x * RB, D)
-        )
-
-    first_step = reduce_first(first_piece, ("yh", "yl"))
+    first_z = lax.psum_scatter(first_sum, "z", scatter_dimension=0, tiled=True)
     grad_bhid = in_order(core, hid_bias[0], hid_bias[1], 1)
     d_shift_two = jnp.sum(d_h_two, axis=0)
     d_scale_two = jnp.sum(d_h_two * norm_two, axis=0)
@@ -585,40 +490,14 @@
     d_attn_low = after(d_attn.astype(BF), first_sum)
     grad_bout = jnp.sum(d_attn, axis=0)
     d_att = [dot(d_attn_low, weight[:, 3 * half :], 1, 0).astype(BF) for weight in attn_halves]
-    d_proj = attend_back(qkv, lax.optimization_barrier(tuple(d_att) + tuple(first_step))[:2])
-    first_y = reduce_rest(first_piece, ("yh", "yl"), first_step).astype(BF)
-    attn_sum = chip_sum(
-        [
-            jnp.concatenate(
-                [dot(h_one, d, 0, 0).astype(BF), dot(d_attn_low, att, 0, 0).astype(BF)], axis=1
-            )
-            for d, att in zip(d_proj, attended)
-        ]
-    )
-    attn_parts = attn_sum.reshape(2 * n_z, n_x, RB, wide)
-
-    def attn_piece(r):
-        return lax.dynamic_slice_in_dim(attn_parts, lax.rem(x_at + r, n_x), 1, axis=1)
-
-    attn_step = reduce_first(attn_piece, "x")
+    d_proj = all_after(attend_back(qkv, d_att), second_z)
     d_h_one = sum(
         dot(d, weight[:, : 3 * half], 1, 1) for d, weight in zip(d_proj, attn_halves)
-    )
-    first_back = exchange(
-        after(first_y.reshape(n_z * n_x, RB, D), attn_sum), ("z", "x")
-    )
-    second_back = exchange(
-        jnp.stack([second_z[..., :D], second_z[..., D:]], axis=1).reshape(4 * n_x, RB, D), PLANE
     )
     qv_bias = [
         jnp.sum(d.astype(F32), axis=0).reshape(2, 3, quarter)[:, ::2].transpose(1, 0, 2)[:, :, None]
         for d in d_proj
     ]
-    attn_x = reduce_rest(attn_piece, "x", attn_step).astype(BF).reshape(2 * n_z, RB, wide)
-    attn_back = exchange(
-        jnp.stack([split_y(attn_x, 0), split_y(attn_x, 1)], axis=1).reshape(4 * n_z, RB, D),
-        ("z", "yh", "yl"),
-    )
     grad_bqv = in_order(core, qv_bias[0], qv_bias[1], 2).reshape(2, D)
     d_shift_one = jnp.sum(d_h_one, axis=0)
     d_scale_one = jnp.sum(d_h_one * norm_one, axis=0)
@@ -639,11 +518,36 @@
     )
 
     lanes = 128
+    small = jnp.concatenate(
+        [
+            grad_bpatch[None],
+            d_mods,
+            grad_bqv,
+            grad_bout[None],
+            grad_bhid,
+            grad_bfc[None],
+            grad_patch,
+            grad_head,
+        ],
+        axis=0,
+    )
+    n_small = small.shape[0]
+    small = jnp.pad(small, ((0, lanes - n_small), (0, 0))).T.astype(BF)
     tiles = 2 * D // lanes
     dmod_sent = jnp.broadcast_to(
         d_mods.astype(BF).reshape(1, 4, tiles, lanes), (n_shard, 4, tiles, lanes)
     ).reshape(n_all, tiles, lanes)
     dmod_all = exchange(dmod_sent, ALL)
+    held = all_after(tuple(d_proj), small)
+    grads = [
+        jnp.concatenate(
+            [dot(h_one, d, 0, 0).astype(BF), dot(d_attn_low, att, 0, 0).astype(BF), small], axis=1
+        )
+        for d, att in zip(held, attended)
+    ]
+    attn_sum = after(chip_sum(grads), first_z, dmod_all)
+    attn_z = lax.psum_scatter(attn_sum, "z", scatter_dimension=0, tiled=True)
+
     mod_sub = lax.dynamic_slice_in_dim(mod_own, 2 * sub, 2, axis=0)
     act_rows = lax.dynamic_slice_in_dim(act_t, shard * RB, RB, axis=0)
     dmod_all = dmod_all.reshape(n_all, 2 * D)
@@ -666,33 +570,34 @@
         [dot(d_pre_time.astype(BF), freq_t, 1, 1), dot(hid_t, d_cond_t, 1, 1)], axis=1
     )
 
-    small = jnp.concatenate(
+    mod_c = in_order(core, grad_mod, swap(grad_mod, "c"), 0)
+    mod_s = in_order(yl, mod_c, swap(mod_c, "yl"), 0)
+    rows = (2 * n_x, RB, -1)
+    attn_z, first_z, second_z = attn_z.reshape(rows), first_z.reshape(rows), second_z.reshape(rows)
+    plane_sent = jnp.stack(
         [
-            grad_bpatch[None],
-            d_mods,
-            grad_bqv,
-            grad_bout[None],
-            grad_bhid,
-            grad_bfc[None],
-            grad_patch,
-            grad_head,
+            jnp.concatenate(
+                [
+                    split_y(attn_z[..., :wide], side),
+                    first_z[..., side * D : (side + 1) * D],
+                    second_z[..., side * D : (side + 1) * D],
+                    attn_z[..., wide:],
+                ],
+                axis=-1,
+            )
+            for side in range(2)
         ],
-        axis=0,
-    )
-    n_small = small.shape[0]
-    small_sent = jnp.pad(small, ((0, lanes - n_small), (0, 0))).T.reshape(n_all, vec_cols, lanes)
-    small_own = jnp.sum(exchange(small_sent, ALL), axis=0).T
+        axis=1,
+    ).reshape(4 * n_x, RB, 3 * D + lanes)
+    plane_own = jnp.sum(exchange(plane_sent, PLANE).astype(F32), axis=0)
+    attn_q = plane_own[:, :D]
+    mlp_q = jnp.stack([plane_own[:, D : 2 * D], plane_own[:, 2 * D : 3 * D]])
+    small_own = lax.dynamic_slice_in_dim(plane_own[:, 3 * D :], sub * vec_cols, vec_cols, axis=0).T
     vec_s = jnp.concatenate(
         [small_own[:1], grad_bt_one[None], grad_bt_two[None], small_own[1:17]], axis=0
     )
     io_s = small_own[17:n_small].reshape(2, PATCH, vec_cols)
 
-    mod_c = in_order(core, grad_mod, swap(grad_mod, "c"), 0)
-    mod_s = in_order(yl, mod_c, swap(mod_c, "yl"), 0)
-    attn_q = jnp.sum(attn_back.astype(F32), axis=0)
-    mlp_q = jnp.stack(
-        [jnp.sum(first_back.astype(F32), axis=0), jnp.sum(second_back.astype(F32), axis=0)]
-    )
     grads_square = jnp.sum(attn_q * attn_q) + jnp.sum(mlp_q * mlp_q)
     attn_q = attn_q.reshape(RB, 4, quarter).transpose(1, 0, 2)
     attn_s = in_order(core, attn_q, swap(attn_q, "c"), 2)
@@ -798,9 +703,9 @@
     )
 
 
-def chip_sum(halves):
+def chip_sum(halves, *between):
     mine, other = halves
-    return (mine.astype(F32) + swap(other, "c").astype(F32)).astype(BF)
+    return (mine.astype(F32) + after(swap(other, "c"), *between).astype(F32)).astype(BF)
 
 
 def solution(mesh):

time: 639 us -> 571 us (0.89)
  starting transfers between devices: 190 us -> 83.9 us
  waiting for transfers between devices: 128 us -> 234 us
  local copies, waits for them, and re-layouts: 89.9 us -> 34.5 us
  blocking collectives: 0 us -> 29 us
  other arithmetic: 74.4 us -> 48 us
  matrix products: 90.7 us -> 77.6 us
    ppermute x37 -> x0, starting transfers between devices: 63.1 us -> none  [shift(): return lax.ppermute(v, axes, [(i, (i + by) % size) for i in range(size)])]
    reduce_scatter x0 -> x2, waiting for transfers between devices: none -> 62.4 us  [the longest x1 52.1 us: on_device(): attn_z = lax.psum_scatter(attn_sum, 'z', scatter_dimension=0, tiled=True)]
    all_to_all x11 -> x8, starting transfers between devices: 111 us -> 72.5 us  [exchange(): return lax.all_to_all(v, axes, 0, 0)]
    all_to_all x11 -> x8, waiting for transfers between devices: 77.1 us -> 111 us  [exchange(): return lax.all_to_all(v, axes, 0, 0)]
    all_gather x1 -> x2, waiting for transfers between devices: 0.02 us -> 32 us  [the longest x1 32 us: on_device(): lax.all_gather(jnp.concatenate([low[..., D:2 * D], high[..., D:2 * D], lo...]
    all_to_all x0 -> x1, blocking collectives: none -> 29 us  [exchange(): return lax.all_to_all(v, axes, 0, 0)]
    ppermute x37 -> x0, waiting for transfers between devices: 26.7 us -> none  [shift(): return lax.ppermute(v, axes, [(i, (i + by) % size) for i in range(size)])]
    dynamic_update_slice x13 -> x0, local copies, waits for them, and re-layouts: 17.2 us -> none  [the longest x6 10.2 us: placed(): out = lax.dynamic_update_slice_in_dim(out, block, where, axis)]
  transfers between devices with their start and end apart: 64 -> 26, of which waited for: 19 -> 14; matrix products, arithmetic and copies ran while one was open for 34% -> 22% of each run, Pallas kernels for 3% -> 3%
where the time goes in v2:
time: 571 us; the launch traced here: 561 us
  waiting for transfers between devices  234 us (41%)
  starting transfers between devices  83.9 us (15%)
  matrix products  77.6 us (14%)
  other arithmetic  48 us (8%)
  local copies, waits for them, and re-layouts  34.5 us (6%)
  between operations  30.2 us (5%)
  blocking collectives  29 us (5%)
  Pallas kernels  23.4 us (4%)
    all_to_all x8, waiting for transfers between devices, exchange(): return lax.all_to_all(v, axes, 0, 0)  111 us
    dot_general x46, matrix products, dot(): lax.dot_general(lhs, rhs, (((lhs_dim,), (rhs_dim,)), ((), ())), precision...  76.2 us
    all_to_all x8, starting transfers between devices, exchange(): return lax.all_to_all(v, axes, 0, 0)  72.5 us
    reduce_scatter x1, waiting for transfers between devices, on_device(): attn_z = lax.psum_scatter(attn_sum, 'z', scatter_dimension=0, tiled=True)  52.1 us
    all_gather x1, waiting for transfers between devices, on_device(): lax.all_gather(jnp.concatenate([low[..., D:2 * D], high[..., D:2 * D], lo...  32 us
    all_to_all x1, blocking collectives, exchange(): return lax.all_to_all(v, axes, 0, 0)  29 us
    ppermute x13, waiting for transfers between devices, swap(): return lax.ppermute(v, axis, [(0, 1), (1, 0)])  22.2 us
    convert_element_type x3, other arithmetic, chip_sum(): (mine.astype(F32) + after(swap(other, 'c'), *between).astype(F32)).astype...  14.5 us
  transfers between devices with their start and end apart: 26, of which 14 were waited for; matrix products, arithmetic and copies ran while one was open for 22% of the time, Pallas kernels for 3%

profile of v2, /device:TPU:1, one launch (start us, length us, event | category | flops | bytes accessed | tf_op | source)
XLA Modules:
  0.0 561.0 jit_solution(4470500421866811440)
XLA Ops:
  9.4 29.0 %all_to_all.45 = bf16[16,16,3072]{2,1,0:T(8,128)(2,1)S(1)} all-to-all(bf16[16,16,3072]{2,1,0:T(8,128)(2,1)S(1)} %broadcast_in_dim.78), channel_id=1, replica_groups=mesh['z'=8,'yh'=2,'x'=4,'yl'=2,'c'=2] {'yh','x','yl'}, dimensions={0} | all-to-all | bytes 3145728 | tf_op jit(solution)/shard_map/all_to_all | solution.py:60
  50.4 12.7 %all-to-all-start = ((bf16[256,4,128]{2,1,0:T(4,128)(2,1)}), bf16[256,4,128]{2,1,0:T(4,128)(2,1)S(1)}, u32[]{:S(2)}, u32[]{:S(2)}) async-start(bf16[256,4,128]{2,1,0:T(4,128)(2,1)} %maximum_maximum_fusion), calls=%async_computation | async-start | bytes 524288 | tf_op jit(solution)/shard_map/all_to_all | solution.py:60
  64.0 16.7 %all-to-all-done = bf16[256,4,128]{2,1,0:T(4,128)(2,1)S(1)} async-done(((bf16[256,4,128]{2,1,0:T(4,128)(2,1)}), bf16[256,4,128]{2,1,0:T(4,128)(2,1)S(1)}, u32[]{:S(2)}, u32[]{:S(2)}) %all-to-all-start) | async-done | bytes 262176 | tf_op jit(solution)/shard_map/all_to_all | solution.py:60
  83.0 5.3 all-to-all-start.1
  90.2 13.1 %all-to-all-done.1 = f32[64,4,256]{2,1,0:T(4,128)S(1)} async-done(((f32[64,4,256]{2,1,0:T(4,128)}), f32[64,4,256]{2,1,0:T(4,128)S(1)}, u32[]{:S(2)}, u32[]{:S(2)}) %all-to-all-start.1) | async-done | bytes 262176 | tf_op jit(solution)/shard_map/all_to_all | solution.py:60
  105.2 9.8 %all-to-all-start.2 = ((bf16[256,4,256]{2,1,0:T(4,128)(2,1)}), bf16[256,4,256]{2,1,0:T(4,128)(2,1)}, u32[]{:S(2)}, u32[]{:S(2)}) async-start(bf16[256,4,256]{2,1,0:T(4,128)(2,1)} %broadcast_in_dim.77), calls=%async_computation.2 | async-start | bytes 1048576 | tf_op jit(solution)/shard_map/all_to_all | solution.py:60
  116.0 21.2 %all-to-all-done.2 = bf16[256,4,256]{2,1,0:T(4,128)(2,1)} async-done(((bf16[256,4,256]{2,1,0:T(4,128)(2,1)}), bf16[256,4,256]{2,1,0:T(4,128)(2,1)}, u32[]{:S(2)}, u32[]{:S(2)}) %all-to-all-start.2) | async-done | bytes 524320 | tf_op jit(solution)/shard_map/all_to_all | solution.py:60
  142.5 5.9 %all-to-all-start.4 = ((f32[256,1,32]{2,1,0:T(1,128)}), f32[256,1,32]{2,1,0:T(1,128)S(1)}, u32[]{:S(2)}, u32[]{:S(2)}) async-start(f32[256,1,32]{2,1,0:T(1,128)} %copy.285), calls=%async_computation.4 | async-start | bytes 262144 | tf_op jit(solution)/shard_map/all_to_all | solution.py:60
  148.6 13.8 %all-to-all-done.4 = f32[256,1,32]{2,1,0:T(1,128)S(1)} async-done(((f32[256,1,32]{2,1,0:T(1,128)}), f32[256,1,32]{2,1,0:T(1,128)S(1)}, u32[]{:S(2)}, u32[]{:S(2)}) %all-to-all-start.4) | async-done | bytes 32800 | tf_op jit(solution)/shard_map/all_to_all | solution.py:60
  165.0 4.0 fusion.28.refs_0_.refs_1_.refs_2_
  169.0 3.8 fusion.31.refs_3_.refs_4_.refs_5_.refs_6_
  172.9 6.4 %shard_map.440 = (bf16[256,512]{1,0:T(8,128)(2,1)}, bf16[256,512]{1,0:T(8,128)(2,1)}) custom-call(bf16[256,1536]{1,0:T(8,128)(2,1)} %fusion.28.refs_0_.refs_1_.refs_2_, bf16[256,1536]{1,0:T(8,128)(2,1)} %fusion.28.refs_0_.refs_1_.refs_2_, bf16[256,1536]{1,0:T(8,128)(2,1)} %fusion.28.refs_0_.refs_1_.refs_2_, ...), custom_call_target="tpu_custom_call" | custom-call | flops 536870912 | bytes 2097152 | tf_op jit(solution)/shard_map/pallas_call | solution.py:251
  179.3 32.0 %all-gather.5.cloned.1.call-done = bf16[1024,4096]{1,0:T(8,128)(2,1)} async-done(((bf16[128,4096]{1,0:T(8,128)(2,1)}), bf16[1024,4096]{1,0:T(8,128)(2,1)}) %all-gather.5.cloned.1.call-update) | async-done | bytes 8388624 | tf_op jit(solution)/shard_map/all_gather | solution.py:332
  228.4 4.6 fusion.147
  242.7 4.8 fusion
  247.5 4.0 add_convert_fusion.2
  259.2 4.1 fusion.142
  268.0 4.0 multiply_reduce_fusion.2
  275.2 6.1 %add_convert_fusion.1 = bf16[1024,2048]{1,0:T(8,128)(2,1)} fusion(bf16[1024,2048]{1,0:T(8,128)(2,1)} %collective-permute-done.3, bf16[1024,2048]{1,0:T(8,128)(2,1)S(1)} %fusion.77), kind=kLoop, calls=%fused_computation.1 | loop fusion | flops 8388608 | bytes 12582912 | tf_op jit(solution)/shard_map/convert_element_type | solution.py:708
  286.7 11.5 %shard_map.441 = (bf16[256,1536]{1,0:T(8,128)(2,1)}, bf16[256,1536]{1,0:T(8,128)(2,1)}) custom-call(bf16[256,1536]{1,0:T(8,128)(2,1)} %fusion.28.refs_0_.refs_1_.refs_2_, bf16[256,1536]{1,0:T(8,128)(2,1)} %fusion.28.refs_0_.refs_1_.refs_2_, bf16[256,1536]{1,0:T(8,128)(2,1)} %fusion.28.refs_0_.refs_1_.refs_2_, ...), custom_call_target="tpu_custom_call" | custom-call | flops 1342177280 | bytes 3670016 | tf_op jit(solution)/shard_map/pallas_call | solution.py:268
  298.2 6.6 %reduce-scatter.4.cloned.1.call-done = bf16[128,2048]{1,0:T(8,128)(2,1)} async-done(((bf16[1024,2048]{1,0:T(8,128)(2,1)}), bf16[128,2048]{1,0:T(8,128)(2,1)}) %reduce-scatter.4.cloned.1.call-update) | async-done | bytes 524304 | tf_op jit(solution)/shard_map/reduce_scatter | solution.py:472
  321.4 9.9 %all-to-all-start.5 = ((bf16[256,16,128]{2,1,0:T(8,128)(2,1)}), bf16[256,16,128]{2,1,0:T(8,128)(2,1)S(1)}, u32[]{:S(2)}, u32[]{:S(2)}) async-start(bf16[256,16,128]{2,1,0:T(8,128)(2,1)} %bitcast.41), calls=%async_computation.7 | async-start | bytes 2097152 | tf_op jit(solution)/shard_map/all_to_all | solution.py:60
  332.9 4.4 add_convert_fusion
  337.3 36.0 %all-to-all-done.5 = bf16[256,16,128]{2,1,0:T(8,128)(2,1)S(1)} async-done(((bf16[256,16,128]{2,1,0:T(8,128)(2,1)}), bf16[256,16,128]{2,1,0:T(8,128)(2,1)S(1)}, u32[]{:S(2)}, u32[]{:S(2)}) %all-to-all-start.5) | async-done | bytes 1048608 | tf_op jit(solution)/shard_map/all_to_all | solution.py:60
  373.3 10.3 %reduce-scatter.6.cloned.1.call-done = bf16[128,2048]{1,0:T(8,128)(2,1)} async-done(((bf16[1024,2048]{1,0:T(8,128)(2,1)}), bf16[128,2048]{1,0:T(8,128)(2,1)}) %reduce-scatter.6.cloned.1.call-update) | async-done | bytes 524304 | tf_op jit(solution)/shard_map/reduce_scatter | solution.py:483
  391.4 10.1 %all-to-all-start.7 = ((bf16[256,4,256]{2,1,0:T(4,128)(2,1)}), bf16[256,4,256]{2,1,0:T(4,128)(2,1)S(1)}, u32[]{:S(2)}, u32[]{:S(2)}) async-start(bf16[256,4,256]{2,1,0:T(4,128)(2,1)} %broadcast_in_dim.180), calls=%async_computation.10 | async-start | bytes 1048576 | tf_op jit(solution)/shard_map/all_to_all | solution.py:60
  401.6 52.1 %reduce-scatter.8.cloned.1.call-done = bf16[128,2176]{1,0:T(8,128)(2,1)} async-done(((bf16[1024,2176]{1,0:T(8,128)(2,1)}), bf16[128,2176]{1,0:T(8,128)(2,1)}) %reduce-scatter.8.cloned.1.call-update) | async-done | bytes 557072 | tf_op jit(solution)/shard_map/reduce_scatter | solution.py:549
  457.8 6.7 %all-to-all-start.6 = ((bf16[16,16,3200]{2,1,0:T(8,128)(2,1)}), bf16[16,16,3200]{2,1,0:T(8,128)(2,1)S(1)}, u32[]{:S(2)}, u32[]{:S(2)}) async-start(bf16[16,16,3200]{2,1,0:T(8,128)(2,1)} %bitcast.48), calls=%async_computation.9 | async-start | bytes 3276800 | tf_op jit(solution)/shard_map/all_to_all | solution.py:60
  470.5 18.7 %collective-permute-done.6 = f32[4,16,1024]{2,1,0:T(8,128)S(1)} collective-permute-done((f32[4,16,1024]{2,1,0:T(8,128)S(1)}, f32[4,16,1024]{2,1,0:T(8,128)S(1)}, u32[]{:S(2)}, u32[]{:S(2)}) %collective-permute-start.6) | collective-permute-done | bytes 262176 | tf_op jit(solution)/shard_map/ppermute | solution.py:72
  500.6 12.1 %all-to-all-start.8 = ((f32[256,1,128]{2,1,0:T(1,128)}), f32[256,1,128]{2,1,0:T(1,128)S(1)}, u32[]{:S(2)}, u32[]{:S(2)}) async-start(f32[256,1,128]{2,1,0:T(1,128)} %broadcast_in_dim.185), calls=%async_computation.11 | async-start | bytes 262144 | tf_op jit(solution)/shard_map/all_to_all | solution.py:60
  515.1 10.3 %all-to-all-done.8 = f32[256,1,128]{2,1,0:T(1,128)S(1)} async-done(((f32[256,1,128]{2,1,0:T(1,128)}), f32[256,1,128]{2,1,0:T(1,128)S(1)}, u32[]{:S(2)}, u32[]{:S(2)}) %all-to-all-start.8) | async-done | bytes 131104 | tf_op jit(solution)/shard_map/all_to_all | solution.py:60
  538.8 5.5 shard_map.442
  (504 shorter events, 135.4 us)
Async XLA Ops:
  7.2 56.0 %copy-start = (bf16[4,4096]{1,0:T(4,128)(2,1)S(1)}, bf16[4,4096]{1,0:T(4,128)(2,1)}, u32[]{:S(2)}) copy-start(bf16[4,4096]{1,0:T(4,128)(2,1)} %param.25) | copy-start | bytes 98308
  7.2 130.0 %all-gather.3.cloned.1.call-start = ((), (), s32[]{:S(2)}) async-start(), calls=%async_computation.12 | async-start | bytes 4718592 | tf_op jit(solution)/shard_map/all_gather | solution.py:329
  39.5 171.9 %all-gather.5.cloned.1.call-start = ((), (), s32[]{:S(2)}) async-start(), calls=%async_computation.13 | async-start | bytes 9437184 | tf_op jit(solution)/shard_map/all_gather | solution.py:332
  50.4 30.3 %all-to-all-start = ((bf16[256,4,128]{2,1,0:T(4,128)(2,1)}), bf16[256,4,128]{2,1,0:T(4,128)(2,1)S(1)}, u32[]{:S(2)}, u32[]{:S(2)}) async-start(bf16[256,4,128]{2,1,0:T(4,128)(2,1)} %maximum_maximum_fusion), calls=%async_computation | async-start | bytes 524288 | tf_op jit(solution)/shard_map/all_to_all | solution.py:60
  83.0 20.3 %all-to-all-start.1 = ((f32[64,4,256]{2,1,0:T(4,128)}), f32[64,4,256]{2,1,0:T(4,128)S(1)}, u32[]{:S(2)}, u32[]{:S(2)}) async-start(f32[64,4,256]{2,1,0:T(4,128)} %copy.280), calls=%async_computation.1 | async-start | bytes 524288 | tf_op jit(solution)/shard_map/all_to_all | solution.py:60
  105.2 32.0 %all-to-all-start.2 = ((bf16[256,4,256]{2,1,0:T(4,128)(2,1)}), bf16[256,4,256]{2,1,0:T(4,128)(2,1)}, u32[]{:S(2)}, u32[]{:S(2)}) async-start(bf16[256,4,256]{2,1,0:T(4,128)(2,1)} %broadcast_in_dim.77), calls=%async_computation.2 | async-start | bytes 1048576 | tf_op jit(solution)/shard_map/all_to_all | solution.py:60
  137.2 31.8 %collective-permute-start = (bf16[1024,2048]{1,0:T(8,128)(2,1)}, bf16[1024,2048]{1,0:T(8,128)(2,1)}, u32[]{:S(2)}, u32[]{:S(2)}) collective-permute-start(bf16[1024,2048]{1,0:T(8,128)(2,1)} %all-gather.3.cloned.1.call-done), channel_id=1, source_target_pairs={{0,1},{1,0},{2,3},{3,2},{4,5},{5,4},{6,7},{7,6},{8,9},{9,8},{10,11... | collective-permute-start | bytes 12582920 | tf_op jit(solution)/shard_map/ppermute | solution.py:72
  142.5 19.9 %all-to-all-start.4 = ((f32[256,1,32]{2,1,0:T(1,128)}), f32[256,1,32]{2,1,0:T(1,128)S(1)}, u32[]{:S(2)}, u32[]{:S(2)}) async-start(f32[256,1,32]{2,1,0:T(1,128)} %copy.285), calls=%async_computation.4 | async-start | bytes 262144 | tf_op jit(solution)/shard_map/all_to_all | solution.py:60
  148.4 156.3 %reduce-scatter.4.cloned.1.call-start = ((), (), s32[]{:S(2)}) async-start(), calls=%async_computation.14 | async-start | bytes 4718592 | tf_op jit(solution)/shard_map/reduce_scatter | solution.py:472
  211.3 13.6 %collective-permute-start.1 = (bf16[1024,4096]{1,0:T(8,128)(2,1)}, bf16[1024,4096]{1,0:T(8,128)(2,1)}, u32[]{:S(2)}, u32[]{:S(2)}) collective-permute-start(bf16[1024,4096]{1,0:T(8,128)(2,1)} %all-gather.5.cloned.1.call-done), channel_id=1, source_target_pairs={{0,1},{1,0},{2,3},{3,2},{4,5},{5,4},{6,7},{7,6},{8,9},{9,8},{10,11... | collective-permute-start | bytes 25165832 | tf_op jit(solution)/shard_map/ppermute | solution.py:72
  238.0 9.4 %collective-permute-start.2 = (bf16[1024,2048]{1,0:T(8,128)(2,1)S(1)}, bf16[1024,2048]{1,0:T(8,128)(2,1)S(1)}, u32[]{:S(2)}, u32[]{:S(2)}) collective-permute-start(bf16[1024,2048]{1,0:T(8,128)(2,1)S(1)} %convolution_convert_fusion.3), channel_id=1, source_target_pairs={{0,1},{1,0},{2,3},{3,2},{4,5},{5,4},{6,7},{7,6},{8,9},{9,8},{10,11... | collective-permute-start | bytes 12582920 | tf_op jit(solution)/shard_map/ppermute | solution.py:72
  251.5 132.1 %reduce-scatter.6.cloned.1.call-start = ((), (), s32[]{:S(2)}) async-start(), calls=%async_computation.15 | async-start | bytes 4718592 | tf_op jit(solution)/shard_map/reduce_scatter | solution.py:483
  258.6 16.6 %collective-permute-start.3 = (bf16[1024,2048]{1,0:T(8,128)(2,1)}, bf16[1024,2048]{1,0:T(8,128)(2,1)}, u32[]{:S(2)}, u32[]{:S(2)}) collective-permute-start(bf16[1024,2048]{1,0:T(8,128)(2,1)} %convolution_convert_fusion.2), channel_id=1, source_target_pairs={{0,1},{1,0},{2,3},{3,2},{4,5},{5,4},{6,7},{7,6},{8,9},{9,8},{10,11... | collective-permute-start | bytes 12582920 | tf_op jit(solution)/shard_map/ppermute | solution.py:72
  259.0 56.4 %copy-start.45 = (bf16[1,1024]{1,0:T(2,128)(2,1)}, bf16[1,1024]{1,0:T(2,128)(2,1)S(1)}, u32[]{:S(2)}) copy-start(bf16[1,1024]{1,0:T(2,128)(2,1)S(1)} %reshape.599) | copy-start | bytes 6148
  259.0 56.4 %copy-start.47 = (bf16[1,1024]{1,0:T(2,128)(2,1)}, bf16[1,1024]{1,0:T(2,128)(2,1)S(1)}, u32[]{:S(2)}) copy-start(bf16[1,1024]{1,0:T(2,128)(2,1)S(1)} %reshape.600) | copy-start | bytes 6148
  259.0 56.4 %copy-start.49 = (bf16[1,1024]{1,0:T(2,128)(2,1)}, bf16[1,1024]{1,0:T(2,128)(2,1)S(1)}, u32[]{:S(2)}) copy-start(bf16[1,1024]{1,0:T(2,128)(2,1)S(1)} %reshape.601) | copy-start | bytes 6148
  319.4 13.5 %collective-permute-start.4 = (bf16[1024,2176]{1,0:T(8,128)(2,1)}, bf16[1024,2176]{1,0:T(8,128)(2,1)}, u32[]{:S(2)}, u32[]{:S(2)}) collective-permute-start(bf16[1024,2176]{1,0:T(8,128)(2,1)} %pad_maximum_fusion), channel_id=1, source_target_pairs={{0,1},{1,0},{2,3},{3,2},{4,5},{5,4},{6,7},{7,6},{8,9},{9,8},{10,11... | collective-permute-start | bytes 13369352 | tf_op jit(solution)/shard_map/ppermute | solution.py:72
  321.4 51.8 %all-to-all-start.5 = ((bf16[256,16,128]{2,1,0:T(8,128)(2,1)}), bf16[256,16,128]{2,1,0:T(8,128)(2,1)S(1)}, u32[]{:S(2)}, u32[]{:S(2)}) async-start(bf16[256,16,128]{2,1,0:T(8,128)(2,1)} %bitcast.41), calls=%async_computation.7 | async-start | bytes 2097152 | tf_op jit(solution)/shard_map/all_to_all | solution.py:60
  331.4 122.3 %reduce-scatter.8.cloned.1.call-start = ((), (), s32[]{:S(2)}) async-start(), calls=%async_computation.16 | async-start | bytes 5013504 | tf_op jit(solution)/shard_map/reduce_scatter | solution.py:549
  384.8 1.5 collective-permute-start.7
  386.3 4.0 collective-permute-start.8
  388.8 66.8 %copy-start.30 = (bf16[128,2048]{1,0:T(8,128)(2,1)S(1)}, bf16[128,2048]{1,0:T(8,128)(2,1)}, u32[]{:S(2)}) copy-start(bf16[128,2048]{1,0:T(8,128)(2,1)} %reduce-scatter.6.cloned.1.call-done) | copy-start | bytes 1572868
  390.3 65.4 %copy-start.29 = (bf16[128,2048]{1,0:T(8,128)(2,1)S(1)}, bf16[128,2048]{1,0:T(8,128)(2,1)}, u32[]{:S(2)}) copy-start(bf16[128,2048]{1,0:T(8,128)(2,1)} %reduce-scatter.4.cloned.1.call-done) | copy-start | bytes 1572868
  391.4 66.4 %all-to-all-start.7 = ((bf16[256,4,256]{2,1,0:T(4,128)(2,1)}), bf16[256,4,256]{2,1,0:T(4,128)(2,1)S(1)}, u32[]{:S(2)}, u32[]{:S(2)}) async-start(bf16[256,4,256]{2,1,0:T(4,128)(2,1)} %broadcast_in_dim.180), calls=%async_computation.10 | async-start | bytes 1048576 | tf_op jit(solution)/shard_map/all_to_all | solution.py:60
  457.8 35.1 %all-to-all-start.6 = ((bf16[16,16,3200]{2,1,0:T(8,128)(2,1)}), bf16[16,16,3200]{2,1,0:T(8,128)(2,1)S(1)}, u32[]{:S(2)}, u32[]{:S(2)}) async-start(bf16[16,16,3200]{2,1,0:T(8,128)(2,1)} %bitcast.48), calls=%async_computation.9 | async-start | bytes 3276800 | tf_op jit(solution)/shard_map/all_to_all | solution.py:60
  465.6 1.9 collective-permute-start.5
  467.6 21.6 %collective-permute-start.6 = (f32[4,16,1024]{2,1,0:T(8,128)S(1)}, f32[4,16,1024]{2,1,0:T(8,128)S(1)}, u32[]{:S(2)}, u32[]{:S(2)}) collective-permute-start(f32[4,16,1024]{2,1,0:T(8,128)S(1)} %maximum_select_fusion.1), channel_id=1, source_target_pairs={{0,2},{2,0},{1,3},{3,1},{4,6},{6,4},{5,7},{7,5},{8,10},{10,8},{9,1... | collective-permute-start | bytes 786440 | tf_op jit(solution)/shard_map/ppermute | solution.py:72
  495.2 19.8 %collective-permute-start.11 = (f32[2,16,1024]{2,1,0:T(8,128)S(1)}, f32[2,16,1024]{2,1,0:T(8,128)S(1)}, u32[]{:S(2)}, u32[]{:S(2)}) collective-permute-start(f32[2,16,1024]{2,1,0:T(8,128)S(1)} %get-tuple-element.358), channel_id=1, source_target_pairs={{0,2},{2,0},{1,3},{3,1},{4,6},{6,4},{5,7},{7,5},{8,10},{10,8},{9,1... | collective-permute-start | bytes 393224 | tf_op jit(solution)/shard_map/ppermute | solution.py:72
  500.6 24.8 %all-to-all-start.8 = ((f32[256,1,128]{2,1,0:T(1,128)}), f32[256,1,128]{2,1,0:T(1,128)S(1)}, u32[]{:S(2)}, u32[]{:S(2)}) async-start(f32[256,1,128]{2,1,0:T(1,128)} %broadcast_in_dim.185), calls=%async_computation.11 | async-start | bytes 262144 | tf_op jit(solution)/shard_map/all_to_all | solution.py:60
  512.8 15.3 %collective-permute-start.9 = (f32[4,16,256]{2,1,0:T(8,128)S(1)}, f32[4,16,256]{2,1,0:T(8,128)S(1)}, u32[]{:S(2)}, u32[]{:S(2)}) collective-permute-start(f32[4,16,256]{2,1,0:T(8,128)S(1)} %bitcast.257), channel_id=1, source_target_pairs={{0,1},{1,0},{2,3},{3,2},{4,5},{5,4},{6,7},{7,6},{8,9},{9,8},{10,11... | collective-permute-start | bytes 196616 | tf_op jit(solution)/shard_map/ppermute | solution.py:72
  528.5 6.9 %collective-permute-start.10 = (f32[4,16,16]{2,1,0:T(8,128)S(1)}, f32[4,16,16]{2,1,0:T(8,128)S(1)}, u32[]{:S(2)}, u32[]{:S(2)}) collective-permute-start(f32[4,16,16]{2,1,0:T(8,128)S(1)} %fusion.161), channel_id=1, source_target_pairs={{0,2},{2,0},{1,3},{3,1},{4,6},{6,4},{5,7},{7,5},{8,10},{10,8},{9,1... | collective-permute-start | bytes 12296 | tf_op jit(solution)/shard_map/ppermute | solution.py:72
  529.1 6.6 %collective-permute-start.12 = (f32[8,16,16]{2,1,0:T(8,128)S(1)}, f32[8,16,16]{2,1,0:T(8,128)S(1)}, u32[]{:S(2)}, u32[]{:S(2)}) collective-permute-start(f32[8,16,16]{2,1,0:T(8,128)S(1)} %fusion.162), channel_id=1, source_target_pairs={{0,1},{1,0},{2,3},{3,2},{4,5},{5,4},{6,7},{7,6},{8,9},{9,8},{10,11... | collective-permute-start | bytes 24584 | tf_op jit(solution)/shard_map/ppermute | solution.py:72
  (93 other events, 1116.0 us)
Sparse Core Ops, SparseCore 0:
  39.6 66.8 all-gather.2
  108.2 103.0 all-gather.4
  251.6 53.0 reduce-scatter.3
  307.1 76.3 reduce-scatter.5
  386.0 67.6 reduce-scatter.7
